TPU v7x, 32 devices: a whole 2x2x4 slice. The times are simulated.
32 devices in a mesh: fsdp: 8 (over z, x), rep: 4 (over y, core).
Axes of the slice: x: 2, y: 2, z: 4, core: 2. Of those that a mesh axis runs over, the one named last changes fastest.
Arguments:
- grad: float32 [4, 256, 8192], P('rep', 'fsdp'), may hold values from -45 to 45
- z_params: float32 [4, 256, 8192], P('rep', 'fsdp'), may hold values from -6 to 6
- x_params: float32 [4, 256, 8192], P('rep', 'fsdp'), may hold values from -6 to 6
- owner: int32 [8], replicated, may hold values from 0 to 7, each once
- stat_left: float32 [8, 1024, 1024], P('fsdp', 'rep'), may hold values from -6 to 6
- stat_right: float32 [8, 1024, 1024], P('fsdp', 'rep'), may hold values from -6 to 6
- root_left: bfloat16 [8, 1024, 1024], P('fsdp', 'rep'), may hold values from -0.1875 to 0.1875
- root_right: bfloat16 [8, 1024, 1024], P('fsdp', 'rep'), may hold values from -0.1875 to 0.1875
Outputs:
- z_new: float32 [4, 256, 8192], P('rep', 'fsdp')
- x_new: float32 [4, 256, 8192], P('rep', 'fsdp')
- y_new: bfloat16 [4, 256, 8192], P('rep', 'fsdp')
- left_new: float32 [8, 1024, 1024], P('fsdp', 'rep')
- right_new: float32 [8, 1024, 1024], P('fsdp', 'rep')
Inputs may be any that keep to these rules, and one draw needn't show every extreme that they name: `owner`: each fsdp index owns exactly one block.
All inputs are finite; a program needn't handle non-finite values.
Results may differ from a plain program's by a relative error of at most 0.0025.
Values may be sent and summed in bfloat16 or wider, within the bound.
No kernel may reach another device: no remote copies, remote signals or barrier semaphores. Data moves between devices by JAX's collectives and lax.ppermute only.
A program may use at most 320 MiB of HBM per device.

v0:
```python
import jax
import jax.numpy as jnp
from jax import lax
from jax.sharding import PartitionSpec as P


def accumulate(carry, piece, start, own_rows, root_rows, member_start):
    left_part, right_part, product, squares = carry
    columns = jnp.dot(own_rows, piece.T, precision=lax.Precision.HIGHEST)
    left_part = lax.dynamic_update_slice_in_dim(left_part, columns, start, 1)
    strip = lax.dynamic_slice_in_dim(piece, member_start, own_rows.shape[0], 1)
    right_part = right_part + jnp.dot(strip.T, piece, precision=lax.Precision.HIGHEST)
    product = jnp.dot(root_rows, piece.astype(jnp.bfloat16), preferred_element_type=jnp.float32)
    squares = squares + jnp.sum(piece * piece)
    return (left_part, right_part, product, squares)


def per_device(grad, z_params, x_params, owner, stat_left, stat_right, root_left, root_right):
    owners = lax.axis_size("fsdp")
    member = lax.axis_index("rep")
    block_size = stat_left.shape[2]
    quarter = stat_left.shape[1]
    member_start = member * quarter
    slots = jnp.arange(owners, dtype=jnp.int32)
    matches = (owner[None, :] == slots[:, None]).astype(jnp.int32)
    inverse = jnp.sum(slots[None, :] * matches, axis=1)
    root_rows = root_left[0]
    zero_block = jnp.zeros((quarter, block_size), jnp.float32)
    start_carry = (zero_block, zero_block, zero_block, jnp.zeros((), jnp.float32))
    flat = grad[0]
    ordered = jnp.take(flat.reshape(flat.shape[0], owners, block_size), inverse, axis=1).reshape(
        flat.shape
    )
    own_rows = lax.all_to_all(
        ordered.astype(jnp.bfloat16), "fsdp", split_axis=1, concat_axis=0, tiled=True
    ).astype(ordered.dtype)
    totals = accumulate(
        start_carry,
        lax.all_gather(own_rows.astype(jnp.bfloat16), "rep", axis=0, tiled=True).astype(
            jnp.float32
        ),
        jnp.int32(0),
        own_rows,
        root_rows,
        member_start,
    )
    left_part, right_part, product, squares = totals
    left_new = 0.95 * stat_left[0] + 0.05 / block_size * left_part
    right_new = 0.95 * stat_right[0] + 0.05 / block_size * right_part
    left_prod = product.astype(jnp.bfloat16)
    precond = jnp.dot(
        left_prod,
        lax.all_gather(root_right[0], "rep", axis=0, tiled=True),
        preferred_element_type=jnp.float32,
    )
    direction_sq = lax.psum(jnp.sum(precond * precond), "rep")
    entries = float(block_size * block_size)
    scale = jnp.sqrt(squares / entries) * lax.rsqrt(direction_sq / entries + 1e-06)
    direction = (scale * precond).astype(jnp.bfloat16)
    returned = lax.all_to_all(direction, "fsdp", split_axis=0, concat_axis=1, tiled=True)
    rows_dev = returned.shape[0]
    flat_dir = jnp.take(returned.reshape(rows_dev, owners, block_size), owner, axis=1).reshape(
        z_params.shape
    )
    z_new = z_params - 0.2 * flat_dir.astype(jnp.float32)
    x_new = 0.75 * x_params + 0.25 * z_new
    y_new = (0.1 * z_new + 0.9 * x_new).astype(jnp.bfloat16)
    return (z_new, x_new, y_new, left_new[None], right_new[None])


def solution(mesh):
    return jax.shard_map(
        per_device,
        mesh=mesh,
        in_specs=(
            P("rep", "fsdp", None),
            P("rep", "fsdp", None),
            P("rep", "fsdp", None),
            P(),
            P("fsdp", "rep", None),
            P("fsdp", "rep", None),
            P("fsdp", "rep", None),
            P("fsdp", "rep", None),
        ),
        out_specs=(
            P("rep", "fsdp", None),
            P("rep", "fsdp", None),
            P("rep", "fsdp", None),
            P("fsdp", "rep", None),
            P("fsdp", "rep", None),
        ),
        check_vma=False,
    )
```

profile of v0, /device:TPU:0, one launch (start us, length us, event | category | flops | bytes accessed | tf_op | source)
XLA Modules:
  0.0 124.3 jit_solution(9584276925557825719)
XLA Ops:
  7.2 0.0 all-gather.4.cloned.1.call-start
  7.2 0.8 select_reduce_fusion
  8.1 1.8 %copy.20 = bf16[4,8,8,1024]{3,2,1,0:T(8,128)(2,1)S(1)} copy(f32[4,8,8,1024]{3,1,2,0:T(8,128)} %bitcast.49) | data formatting | bytes 1572864
  9.9 0.3 copy.17
  10.2 0.6 gather_fusion
  10.8 0.2 fusion.6
  10.9 21.7 %all_to_all.32 = bf16[32,8,1024]{2,0,1:T(8,128)(2,1)} all-to-all(bf16[32,8,1024]{2,0,1:T(8,128)(2,1)S(1)} %fusion.6), channel_id=1, replica_groups=mesh['fsdp'=8,'rep'=4] {'fsdp'}, dimensions={1} | all-to-all | bytes 1048576 | tf_op jit(solution)/shard_map/all_to_all | solution.py:34
  32.7 0.0 all-gather.6.cloned.1.call-start
  32.7 0.7 all-gather.6.cloned.1.call-update
  33.4 0.1 broadcast_bitcast_fusion
  33.5 20.9 %all-gather.4.cloned.1.call-done = bf16[1024,1024]{1,0:T(8,128)(2,1)} async-done(((bf16[256,1024]{1,0:T(8,128)(2,1)}), bf16[1024,1024]{1,0:T(8,128)(2,1)}) %all-gather.4.cloned.1.call-update) | async-done | bytes 2097168 | tf_op jit(solution)/shard_map/all_gather | solution.py:39
  54.5 3.4 %multiply_reduce_fusion = f32[]{:T(128)} fusion(bf16[1024,1024]{1,0:T(8,128)(2,1)} %all-gather.4.cloned.1.call-done), kind=kLoop, calls=%fused_computation.2 | loop fusion | flops 3145727 | bytes 2097156 | tf_op jit(solution)/shard_map/reduce_sum | solution.py:14
  58.6 20.1 %all-gather.6.cloned.1.call-done = bf16[1,1024,1024]{2,1,0:T(8,128)(2,1)} async-done(((bf16[1,256,1024]{2,1,0:T(8,128)(2,1)}), bf16[1,1024,1024]{2,1,0:T(8,128)(2,1)}) %all-gather.6.cloned.1.call-update) | async-done | bytes 2097168 | tf_op jit(solution)/shard_map/all_gather | solution.py:53
  78.6 5.5 %multiply_reduce_fusion.1 = (f32[]{:T(128)}, f32[256,1024]{1,0:T(8,128)}) fusion(bf16[1,1024,1024]{2,1,0:T(8,128)(2,1)} %all-gather.6.cloned.1.call-done, bf16[1024,1024]{1,0:T(8,128)(2,1)S(1)} %copy-done.1, bf16[1,256,1024]{2,1,0:T(8,128)(2,1)S(1)} %copy-done), kind=kOutput, calls=%fused_computation.17 | convolution fusion | flops 1074528256 | bytes 5767172 | tf_op jit(solution)/shard_map/dot_general | solution.py:51
  84.1 6.5 %psum.7 = f32[]{:T(128)} all-reduce(f32[]{:T(128)} %get-tuple-element.8), channel_id=1, replica_groups=mesh['fsdp'=8,'rep'=4] {'rep'}, use_global_device_ids=true, to_apply=%region_3.4 | all-reduce | flops 1 | bytes 8 | tf_op jit(solution)/shard_map/psum | solution.py:56
  91.3 2.1 %multiply_convert_fusion = bf16[256,1024]{1,0:T(8,128)(2,1)} fusion(f32[256,1024]{1,0:T(8,128)} %get-tuple-element.9, f32[]{:T(128)S(6)} %mul.86), kind=kLoop, calls=%fused_computation.16 | loop fusion | flops 524288 | bytes 1572868 | tf_op jit(solution)/shard_map/convert_element_type | solution.py:59
  93.4 5.7 %all-to-all-start.1 = ((bf16[8,32,1024]{2,1,0:T(8,128)(2,1)}), bf16[8,32,1024]{2,1,0:T(8,128)(2,1)S(1)}, u32[]{:S(2)}, u32[]{:S(2)}) async-start(bf16[8,32,1024]{2,1,0:T(8,128)(2,1)} %bitcast.47), calls=%async_computation.1 | async-start | bytes 1048576 | tf_op jit(solution)/shard_map/all_to_all | solution.py:60
  99.1 3.1 %fusion.3 = f32[1,256,1024]{2,1,0:T(8,128)} fusion(bf16[1024,1024]{1,0:T(8,128)(2,1)S(1)} %copy-done.1, f32[1,256,1024]{2,1,0:T(8,128)} %param.13, s32[]{:T(128)S(6)} %select_n.46), kind=kOutput, calls=%fused_computation.7 | convolution fusion | flops 537657344 | bytes 4718596 | tf_op jit(solution)/shard_map/dot_general | solution.py:12
  102.2 1.8 %fusion.5 = f32[1,256,1024]{2,1,0:T(8,128)} fusion(bf16[256,1024]{1,0:T(8,128)(2,1)S(1)} %bitcast.44, bf16[1024,1024]{1,0:T(8,128)(2,1)S(1)} %copy-done.1, f32[1,256,1024]{2,1,0:T(8,128)S(1)} %copy-done.4), kind=kOutput, calls=%fused_computation.10 | convolution fusion | flops 537657344 | bytes 4718592 | tf_op jit(solution)/shard_map/dot_general | solution.py:9
  104.0 9.3 %all-to-all-done.1 = bf16[8,32,1024]{2,1,0:T(8,128)(2,1)S(1)} async-done(((bf16[8,32,1024]{2,1,0:T(8,128)(2,1)}), bf16[8,32,1024]{2,1,0:T(8,128)(2,1)S(1)}, u32[]{:S(2)}, u32[]{:S(2)}) %all-to-all-start.1) | async-done | bytes 524320 | tf_op jit(solution)/shard_map/all_to_all | solution.py:60
  113.3 0.6 gather_fusion.1
  113.9 0.3 copy.18
  114.2 0.2 gather.12
  114.4 3.0 %add_convert_fusion = (bf16[1,32,8192]{2,1,0:T(8,128)(2,1)}, f32[1,32,8192]{2,1,0:T(8,128)}, f32[1,32,8192]{2,1,0:T(8,128)}) fusion(f32[1,32,8192]{2,1,0:T(8,128)S(1)} %copy-done.3, f32[1,32,8192]{2,1,0:T(8,128)} %param.9, bf16[1,32,8192]{2,1,0:T(8,128)(2,1)S(1)} %gather.12, pred[8192]{0:T(1024)(128)(4,1)S(1)} %bitcast.50), kind=kLoop, calls=%fused_computation.13 | loop fusion | flops 2883584 | bytes 5251072 | tf_op jit(solution)/shard_map/convert_element_type | solution.py:67
  (20 shorter events, 0.1 us)
Async XLA Ops:
  7.2 71.5 %copy-start = (bf16[1,256,1024]{2,1,0:T(8,128)(2,1)S(1)}, bf16[1,256,1024]{2,1,0:T(8,128)(2,1)}, u32[]{:S(2)}) copy-start(bf16[1,256,1024]{2,1,0:T(8,128)(2,1)} %param.14) | copy-start | bytes 1572868
  7.2 47.3 %all-gather.4.cloned.1.call-start = ((), (), s32[]{:S(2)}) async-start(), calls=%async_computation.2 | async-start | bytes 2621440 | tf_op jit(solution)/shard_map/all_gather | solution.py:39
  10.2 23.2 %copy-start.5 = (s32[8]{0:T(128)S(1)}, s32[8]{0:T(128)}, u32[]{:S(2)}) copy-start(s32[8]{0:T(128)} %param.11) | copy-start | bytes 100
  32.7 46.0 %all-gather.6.cloned.1.call-start = ((), (), s32[]{:S(2)}) async-start(), calls=%async_computation.3 | async-start | bytes 2621440 | tf_op jit(solution)/shard_map/all_gather | solution.py:53
  54.5 24.2 %copy-start.1 = (bf16[1024,1024]{1,0:T(8,128)(2,1)S(1)}, bf16[1024,1024]{1,0:T(8,128)(2,1)}, u32[]{:S(2)}) copy-start(bf16[1024,1024]{1,0:T(8,128)(2,1)} %all-gather.4.cloned.1.call-done) | copy-start | bytes 6291460
  93.4 19.8 %all-to-all-start.1 = ((bf16[8,32,1024]{2,1,0:T(8,128)(2,1)}), bf16[8,32,1024]{2,1,0:T(8,128)(2,1)S(1)}, u32[]{:S(2)}, u32[]{:S(2)}) async-start(bf16[8,32,1024]{2,1,0:T(8,128)(2,1)} %bitcast.47), calls=%async_computation.1 | async-start | bytes 1048576 | tf_op jit(solution)/shard_map/all_to_all | solution.py:60
  99.1 3.1 %copy-start.2 = (bf16[32,8,1024]{2,0,1:T(8,128)(2,1)S(1)}, bf16[32,8,1024]{2,0,1:T(8,128)(2,1)}, u32[]{:S(2)}) copy-start(bf16[32,8,1024]{2,0,1:T(8,128)(2,1)} %all_to_all.32) | copy-start | bytes 1572868
  99.1 3.1 %copy-start.4 = (f32[1,256,1024]{2,1,0:T(8,128)S(1)}, f32[1,256,1024]{2,1,0:T(8,128)}, u32[]{:S(2)}) copy-start(f32[1,256,1024]{2,1,0:T(8,128)} %param.12) | copy-start | bytes 3145732
  104.0 10.4 %copy-start.3 = (f32[1,32,8192]{2,1,0:T(8,128)S(1)}, f32[1,32,8192]{2,1,0:T(8,128)}, u32[]{:S(2)}) copy-start(f32[1,32,8192]{2,1,0:T(8,128)} %param.10) | copy-start | bytes 3145732
Sparse Core Ops, SparseCore 0:
  32.8 21.6 all-gather.3
  56.0 22.5 all-gather.5
where the time goes:
time: 125 us; the launch traced here: 124 us
  waiting for transfers between devices  51 us (41%)
  blocking collectives  28.2 us (23%)
  between operations  15.6 us (12%)
  matrix products  10.3 us (8%)
  other arithmetic  9.57 us (8%)
  starting transfers between devices  5.74 us (5%)
  local copies, waits for them, and re-layouts  3.9 us (3%)
    all_to_all x1, blocking collectives, per_device(): lax.all_to_all(ordered.astype(jnp.bfloat16), 'fsdp', split_axis=1, concat...  21.7 us
    all_gather x1, waiting for transfers between devices, per_device(): lax.all_gather(own_rows.astype(jnp.bfloat16), 'rep', axis=0, tiled=True)  20.9 us
    all_gather x1, waiting for transfers between devices, per_device(): lax.all_gather(root_right[0], 'rep', axis=0, tiled=True)  20.1 us
    all_to_all x1, waiting for transfers between devices, per_device(): lax.all_to_all(direction, 'fsdp', split_axis=0, concat_axis=1, tiled=True)  9.27 us
    psum x1, blocking collectives, per_device(): direction_sq = lax.psum(jnp.sum(precond * precond), 'rep')  6.5 us
    all_to_all x1, starting transfers between devices, per_device(): lax.all_to_all(direction, 'fsdp', split_axis=0, concat_axis=1, tiled=True)  5.66 us
    dot_general x1, matrix products, per_device(): jnp.dot(left_prod, lax.all_gather(root_right[0], 'rep', axis=0, tiled=Tru...  5.48 us
    reduce_sum x1, other arithmetic, accumulate(): squares = squares + jnp.sum(piece * piece)  3.42 us
  transfers between devices with their start and end apart: 3, of which 3 were waited for; matrix products, arithmetic and copies ran while one was open for 7% of the time, Pallas kernels for 0%

commit v1 on v0

v1 whole, which is shorter than its diff:
```python
import functools

import jax
import jax.numpy as jnp
from jax import lax
from jax.experimental import pallas as pl
from jax.experimental.pallas import tpu as pltpu
from jax.sharding import PartitionSpec as P

F32 = jnp.float32
BF16 = jnp.bfloat16
ANY = pl.BlockSpec(memory_space=pl.ANY)
VMEM = pl.BlockSpec(memory_space=pltpu.VMEM)
HBM = pl.BlockSpec(memory_space=pltpu.HBM)
MIB = 1 << 20


def params(mib):
    return pltpu.CompilerParams(vmem_limit_bytes=mib * MIB)


def cost(flops, moved):
    return pl.CostEstimate(flops=flops, bytes_accessed=moved, transcendentals=0)


def swap(x, axis, size, bit):
    return lax.ppermute(x, axis, [(i, i ^ bit) for i in range(size)])


def in_hbm(x):
    return pltpu.with_memory_space_constraint(x, pltpu.HBM)


def invert(owner_mem, block_mem, count):
    for b in range(count):
        block_mem[owner_mem[b]] = jnp.int32(b)


def route_kernel(owner_ref, grad_ref, *refs):
    outs, (owner_mem, block_mem, held, sems) = refs[:-4], refs[-4:]
    me = lax.axis_index("fsdp")
    count, rows, width = held.shape

    def load(b):
        start = b * width if isinstance(b, int) else pl.multiple_of(b * width, width)
        return pltpu.make_async_copy(
            grad_ref.at[:, pl.ds(start, width)], held.at[b], sems.at[b]
        )

    index = pltpu.make_async_copy(owner_ref, owner_mem, sems.at[count])
    index.start()
    for b in range(count):
        load(b).start()
    index.wait()
    invert(owner_mem, block_mem, count)
    for d in reversed(range(count)):
        b = block_mem[me ^ d]
        load(b).wait()
        outs[d][...] = held[b].astype(BF16)


def route(grad, owner, count):
    rows, width = grad.shape[0], grad.shape[1] // count
    return pl.pallas_call(
        route_kernel,
        out_shape=[jax.ShapeDtypeStruct((rows, width), BF16)] * count,
        in_specs=[HBM, HBM],
        out_specs=[VMEM] * count,
        scratch_shapes=[
            pltpu.SMEM((count,), jnp.int32),
            pltpu.SMEM((count,), jnp.int32),
            pltpu.VMEM((count, rows, width), F32),
            pltpu.SemaphoreType.DMA((count + 1,)),
        ],
        compiler_params=params(8),
        cost_estimate=cost(0, 6 * grad.size),
        name="route",
    )(in_hbm(owner), in_hbm(grad))


def local_call(kernel, shape, operands, name, *early):
    return pl.pallas_call(
        kernel,
        out_shape=jax.ShapeDtypeStruct(shape, BF16),
        in_specs=[VMEM] * len(operands) + [ANY] * len(early),
        out_specs=VMEM,
        compiler_params=params(8),
        cost_estimate=cost(0, 4 * shape[0] * shape[1]),
        name=name,
    )(*operands, *early)


FIRST = (0, 1, 4, 5)
SECOND = (2, 3, 6, 7)


def half_kernel(half_of, there, *refs):
    out_ref = refs[-1]
    rows = refs[0].shape[0]
    odd = lax.axis_index("fsdp") % 2
    for ref, d in zip(refs, there):
        place = half_of.index(d) // 2 * 2 + (odd ^ (d % 2))
        out_ref[pl.ds(pl.multiple_of(place * rows, rows), rows), :] = ref[...]


def half(got, half_of, there, *early):
    rows, width = got[0].shape
    kernel = functools.partial(half_kernel, half_of, there)
    return local_call(kernel, (4 * rows, width), [got[d] for d in there], "half", *early)


def join_kernel(first_ref, second_ref, *refs):
    out_ref = refs[-1]
    rows = first_ref.shape[0] // 2
    pair = lax.axis_index("fsdp") // 2
    for ref, half_of in ((first_ref, FIRST), (second_ref, SECOND)):
        for k in range(2):
            place = pl.multiple_of((pair ^ (half_of[2 * k] // 2)) * rows, rows)
            out_ref[pl.ds(place, rows), :] = ref[k * rows : (k + 1) * rows, :]


def join(first, second, *early):
    shape = (2 * first.shape[0], first.shape[1])
    return local_call(join_kernel, shape, (first, second), "join", *early)


def after(x, first):
    def kernel(x_ref, first_ref, out_ref):
        pass

    return pl.pallas_call(
        kernel,
        out_shape=jax.ShapeDtypeStruct(x.shape, x.dtype),
        in_specs=[ANY, ANY],
        out_specs=ANY,
        input_output_aliases={0: 0},
        compiler_params=params(1),
        cost_estimate=cost(0, 0),
        name="after",
    )(x, first)


def precond_kernel(members, left_ref, *refs):
    g_refs, r_refs = refs[:members], refs[members : 2 * members]
    out_ref, sums_ref, mid_ref = refs[-3:]
    member = lax.axis_index("rep")
    q = left_ref.shape[0]

    def part(ref, j):
        return ref[:, pl.ds(pl.multiple_of((member ^ j) * q, q), q)]

    def chain(ref, rights):
        total = jnp.dot(part(ref, 0), rights[0][...], preferred_element_type=F32)
        for j in range(1, members):
            total += jnp.dot(part(ref, j), rights[j][...], preferred_element_type=F32)
        return total

    mid_ref[...] = chain(left_ref, g_refs).astype(BF16)
    product = chain(mid_ref, r_refs)
    out_ref[...] = product
    own = g_refs[0][...].astype(F32)
    rows = lax.broadcasted_iota(jnp.int32, sums_ref.shape, 0)
    sums_ref[...] = jnp.where(rows == 0, jnp.sum(product * product), jnp.sum(own * own))


def precondition(left, blocks, rights, *early):
    q, width = left.shape
    members = len(blocks)
    return pl.pallas_call(
        functools.partial(precond_kernel, members),
        out_shape=[
            jax.ShapeDtypeStruct((q, width), F32),
            jax.ShapeDtypeStruct((8, 128), F32),
        ],
        in_specs=[VMEM] * (1 + 2 * members) + [ANY] * len(early),
        out_specs=[VMEM, VMEM],
        scratch_shapes=[pltpu.VMEM((q, width), BF16)],
        compiler_params=params(16),
        cost_estimate=cost(4 * q * width * width, 4 * width * width + 4 * q * width),
        name="precondition",
    )(left, *blocks, *rights, *early)


def scale_kernel(entries, count, n, product_ref, *refs):
    sums_refs, outs = refs[:n], refs[-count:]
    me = lax.axis_index("fsdp")
    rows = outs[0].shape[0]
    total = sum(ref[...] for ref in sums_refs) / entries
    scale = jnp.sqrt(total[1:2, :1]) * lax.rsqrt(total[:1, :1] + 1e-06)
    for d, out_ref in enumerate(outs):
        part = product_ref[pl.ds(pl.multiple_of((me ^ d) * rows, rows), rows), :]
        out_ref[...] = (scale * part).astype(BF16)


def rescale(product, sums, entries, count, *early):
    rows, width = product.shape[0] // count, product.shape[1]
    return pl.pallas_call(
        functools.partial(scale_kernel, entries, count, len(sums)),
        out_shape=[jax.ShapeDtypeStruct((rows, width), BF16)] * count,
        in_specs=[VMEM] * (1 + len(sums)) + [HBM] * len(early),
        out_specs=[VMEM] * count,
        compiler_params=params(8),
        cost_estimate=cost(product.size, 6 * product.size),
        name="rescale",
    )(product, *sums, *map(in_hbm, early))


def stats_kernel(members, rows_side, old_ref, *refs):
    g_refs = refs[:members]
    new_out, new_mem, sems = refs[members:]
    member = lax.axis_index("rep")
    q, width = old_ref.shape
    step = 0.05 / width
    strip = pl.ds(pl.multiple_of(member * q, q), q)
    stores = []
    for j in range(members):
        if rows_side:
            cols = pl.ds(pl.multiple_of((member ^ j) * q, q), q)
            product = lax.dot_general(
                g_refs[0][...], g_refs[j][...], (((1,), (1,)), ((), ())), preferred_element_type=F32
            )
        else:
            cols = pl.ds(j * q, q)
            product = sum(
                lax.dot_general(
                    g[:, strip], g[:, cols], (((0,), (0,)), ((), ())), preferred_element_type=F32
                )
                for g in g_refs
            )
        new_mem[j] = 0.95 * old_ref[:, cols] + step * product
        stores.append(pltpu.make_async_copy(new_mem.at[j], new_out.at[:, cols], sems.at[j]))
        stores[-1].start()
    for store in stores:
        store.wait()


def statistic(old, blocks, rows_side):
    q, width = old.shape
    members = len(blocks)
    return pl.pallas_call(
        functools.partial(stats_kernel, members, rows_side),
        out_shape=jax.ShapeDtypeStruct((q, width), F32),
        in_specs=[VMEM] * (1 + members),
        out_specs=HBM,
        scratch_shapes=[
            pltpu.VMEM((members, q, q), F32),
            pltpu.SemaphoreType.DMA((members,)),
        ],
        compiler_params=params(16),
        cost_estimate=cost(2 * q * width * width, 8 * q * width + 2 * width * width),
        name="left_statistic" if rows_side else "right_statistic",
    )(old, *blocks)


def stage_kernel(n, owner_ref, z_ref, x_ref, *refs):
    whole_refs, whole_outs = refs[:n], refs[-n - 6 : -6]
    z_out, x_out, block_out, owner_mem, block_mem, sems = refs[-6:]
    me = lax.axis_index("fsdp")
    count, _, width = z_out.shape
    index = pltpu.make_async_copy(owner_ref, owner_mem, sems.at[2, n])
    index.start()
    loads = [
        pltpu.make_async_copy(src, dst, sems.at[2, i])
        for i, (src, dst) in enumerate(zip(whole_refs, whole_outs))
    ]
    for load in loads:
        load.start()
    index.wait()
    invert(owner_mem, block_mem, count)
    for d in range(count):
        block = block_mem[me ^ d]
        block_out[pl.ds(d, 1), :] = jnp.full((1, block_out.shape[1]), block, jnp.int32)
        cols = pl.ds(pl.multiple_of(block * width, width), width)
        for i, (src, dst) in enumerate(((z_ref, z_out), (x_ref, x_out))):
            load = pltpu.make_async_copy(src.at[:, cols], dst.at[d], sems.at[i, d])
            load.start()
            loads.append(load)
    for load in loads:
        load.wait()


def stage(owner, z, x, wholes, count, *early):
    rows, width = z.shape[0], z.shape[1] // count
    n = len(wholes)
    moved = sum(2 * w.size * w.dtype.itemsize for w in wholes)
    return pl.pallas_call(
        functools.partial(stage_kernel, n),
        out_shape=[jax.ShapeDtypeStruct(w.shape, w.dtype) for w in wholes]
        + [
            jax.ShapeDtypeStruct((count, rows, width), F32),
            jax.ShapeDtypeStruct((count, rows, width), F32),
            jax.ShapeDtypeStruct((count, 128), jnp.int32),
        ],
        in_specs=[HBM] * (3 + n) + [ANY] * len(early),
        out_specs=[VMEM] * (n + 3),
        scratch_shapes=[
            pltpu.SMEM((count,), jnp.int32),
            pltpu.SMEM((count,), jnp.int32),
            pltpu.SemaphoreType.DMA((3, count)),
        ],
        compiler_params=params(8),
        cost_estimate=cost(0, 16 * z.size + moved),
        name="stage",
    )(*[in_hbm(a) for a in (owner, z, x, *wholes)], *early)


def update_kernel(distances, fresh, block_ref, z_ref, x_ref, *refs):
    n = len(distances)
    back, outs = refs[:n], refs[n : n + 3] if fresh else refs[n + 3 : n + 6]
    z_mem, x_mem, y_mem, sems = refs[-4:]
    width = z_ref.shape[2]
    blocks = [block_ref[d, 0] for d in distances]
    stores = []
    for k, d in enumerate(distances):
        z_new = z_ref[d] - 0.2 * back[k][...].astype(F32)
        x_new = 0.75 * x_ref[d] + 0.25 * z_new
        z_mem[k] = z_new
        x_mem[k] = x_new
        y_mem[k] = (0.1 * z_new + 0.9 * x_new).astype(BF16)
        cols = pl.ds(pl.multiple_of(blocks[k] * width, width), width)
        for i, mem in enumerate((z_mem, x_mem, y_mem)):
            store = pltpu.make_async_copy(mem.at[k], outs[i].at[:, cols], sems.at[i, k])
            store.start()
            stores.append(store)
    for store in stores:
        store.wait()


def update(block, z, x, back, distances, held=None):
    count, rows, width = z.shape
    flat = (rows, count * width)
    n = len(distances)
    fresh = held is None
    return pl.pallas_call(
        functools.partial(update_kernel, distances, fresh),
        out_shape=[
            jax.ShapeDtypeStruct(flat, F32),
            jax.ShapeDtypeStruct(flat, F32),
            jax.ShapeDtypeStruct(flat, BF16),
        ],
        in_specs=[VMEM] * (3 + n) + ([] if fresh else [HBM] * 3),
        out_specs=[HBM] * 3,
        input_output_aliases={} if fresh else {3 + n + i: i for i in range(3)},
        scratch_shapes=[
            pltpu.VMEM((n, rows, width), F32),
            pltpu.VMEM((n, rows, width), F32),
            pltpu.VMEM((n, rows, width), BF16),
            pltpu.SemaphoreType.DMA((3, n)),
        ],
        compiler_params=params(16),
        cost_estimate=cost(8 * n * rows * width, 20 * n * rows * width),
        name="update",
    )(block, z, x, *[back[d] for d in distances], *([] if fresh else held))


def gather_members(own, members):
    bit = members // 2
    got = {0: own}
    while bit:
        for known in list(got):
            got[known ^ bit] = swap(got[known], "rep", members, bit)
        bit //= 2
    return [got[j] for j in range(members)]


def eight_by_four(flat, z, x, owner, stat_left, stat_right, root_left, root_right, count, members):
    def send(piece, d):
        return swap(piece, "fsdp", count, d)

    def far(piece):
        return swap(piece, "rep", members, 2)

    def sibling(piece):
        return swap(piece, "rep", members, 1)

    entries = float(stat_left.shape[1] ** 2)
    right_far = far(root_right)
    piece = route(flat, owner, count)
    got = {0: piece[0]}
    for d in (4, 5, 3, 1):
        got[d] = send(piece[d], d)
    got[2] = send(after(piece[2], got[3]), 2)
    got[7] = send(after(piece[7], got[1]), 7)
    got[6] = send(after(piece[6], got[4]), 6)
    first = half(got, FIRST, (4, 5, 1, 0))
    first_far = far(first)
    second = half(got, SECOND, (3, 2, 7, 6))
    second_far = far(second)
    wholes = (root_left, root_right, stat_left, stat_right)
    left, right, stat_left, stat_right, z, x, block = stage(owner, z, x, wholes, count, first, second)
    own = join(first, second, z)
    right_sibling = sibling(right)
    own_sibling = sibling(own)
    first_both, second_both = sibling(first_far), sibling(second_far)
    right_both = sibling(right_far)
    blocks = [own, own_sibling, join(first_far, second_far), join(first_both, second_both)]
    rights = [right, right_sibling, right_far, right_both]
    product, sums = precondition(left, blocks, rights)
    sums = [sums] + [swap(sums, "rep", members, j) for j in (1, 2, 3)]
    left_new = statistic(stat_left, blocks, True)
    piece = rescale(product, sums, entries, count, left_new)
    back = {0: piece[0]}
    for d in (4, 1, 5, 6, 7, 3, 2):
        back[d] = send(piece[d], d)
    new = None
    for distances in ((4, 1, 5, 0), (6, 3), (7, 2)):
        new = update(block, z, x, back, distances, new)
    return (*new, left_new, statistic(stat_right, blocks, False))


def any_shape(flat, z, x, owner, stat_left, stat_right, root_left, root_right, count, members):
    q, width = root_left.shape
    entries = float(width**2)
    rows = flat.shape[0]
    sent = jnp.take(flat.reshape(rows, count, width), jnp.argsort(owner), axis=1)
    sent = sent.transpose(1, 0, 2).astype(BF16)
    own = lax.all_to_all(sent, "fsdp", 0, 0, tiled=True).reshape(q, width)
    blocks = gather_members(own, members)
    rights = gather_members(root_right, members)
    product, sums = precondition(root_left, blocks, rights)
    total = sum([sums] + [swap(sums, "rep", members, j) for j in range(1, members)]) / entries
    scale = jnp.sqrt(total[1, 0]) * lax.rsqrt(total[0, 0] + 1e-06)
    back = (scale * product).astype(BF16).reshape(count, rows, width)
    back = lax.all_to_all(back, "fsdp", 0, 0, tiled=True)
    back = jnp.take(back, owner, axis=0).transpose(1, 0, 2).reshape(z.shape).astype(F32)
    z_new = z - 0.2 * back
    x_new = 0.75 * x + 0.25 * z_new
    y_new = (0.1 * z_new + 0.9 * x_new).astype(BF16)
    return (z_new, x_new, y_new, statistic(stat_left, blocks, True), statistic(stat_right, blocks, False))


def per_device(grad, z_params, x_params, owner, stat_left, stat_right, root_left, root_right):
    count = lax.axis_size("fsdp")
    members = lax.axis_size("rep")
    plan = eight_by_four if (count, members) == (8, 4) else any_shape
    held = (stat_left[0], stat_right[0], root_left[0], root_right[0])
    new = plan(grad[0], z_params[0], x_params[0], owner, *held, count, members)
    return tuple(part[None] for part in new)


def solution(mesh):
    flat = P("rep", "fsdp", None)
    held = P("fsdp", "rep", None)
    return jax.shard_map(
        per_device,
        mesh=mesh,
        in_specs=(flat, flat, flat, P(), held, held, held, held),
        out_specs=(flat, flat, flat, held, held),
        check_vma=False,
    )
```

time: 125 us -> 53.3 us (0.43)
  waiting for transfers between devices: 51 us -> 11.4 us
  blocking collectives: 28.2 us -> 0 us
  starting transfers between devices: 5.74 us -> 28.3 us
  between operations: 15.6 us -> 0.82 us
  Pallas kernels: 0 us -> 12.6 us
  matrix products: 10.3 us -> 0 us
  other arithmetic: 9.57 us -> 0 us
  local copies, waits for them, and re-layouts: 3.9 us -> 0 us
    all_gather x2 -> x0, waiting for transfers between devices: 41 us -> none  [the longest x1 20.9 us: per_device(): lax.all_gather(own_rows.astype(jnp.bfloat16), 'rep', axis=0, tiled=True)]
    ppermute x0 -> x25, starting transfers between devices: none -> 28.3 us  [swap(): return lax.ppermute(x, axis, [(i, i ^ bit) for i in range(size)])]
    all_to_all x1 -> x0, blocking collectives: 21.7 us -> none  [per_device(): lax.all_to_all(ordered.astype(jnp.bfloat16), 'fsdp', split_axis=1, concat...]
    pallas_call x0 -> x17, Pallas kernels: none -> 12.6 us  [the longest x2 3.31 us: statistic(): pl.pallas_call(functools.partial(stats_kernel, members, rows_side), out_s...]
    ppermute x0 -> x25, waiting for transfers between devices: none -> 11.4 us  [swap(): return lax.ppermute(x, axis, [(i, i ^ bit) for i in range(size)])]
    dot_general x3 -> x0, matrix products: 10.3 us -> none  [the longest x1 5.48 us: per_device(): jnp.dot(left_prod, lax.all_gather(root_right[0], 'rep', axis=0, tiled=Tru...]
    all_to_all x1 -> x0, waiting for transfers between devices: 9.27 us -> none  [per_device(): lax.all_to_all(direction, 'fsdp', split_axis=0, concat_axis=1, tiled=True)]
    psum x1 -> x0, blocking collectives: 6.5 us -> none  [per_device(): direction_sq = lax.psum(jnp.sum(precond * precond), 'rep')]
  transfers between devices with their start and end apart: 3 -> 25, of which waited for: 3 -> 9; matrix products, arithmetic and copies ran while one was open for 7% -> 0% of each run, Pallas kernels for 0% -> 19%
where the time goes in v1:
time: 53.3 us; the launch traced here: 53.2 us
  starting transfers between devices  28.3 us (53%)
  Pallas kernels  12.6 us (24%)
  waiting for transfers between devices  11.4 us (21%)
  between operations  0.82 us (2%)
    ppermute x25, starting transfers between devices, swap(): return lax.ppermute(x, axis, [(i, i ^ bit) for i in range(size)])  28.3 us
    ppermute x25, waiting for transfers between devices, swap(): return lax.ppermute(x, axis, [(i, i ^ bit) for i in range(size)])  11.4 us
    pallas_call x2, Pallas kernels, statistic(): pl.pallas_call(functools.partial(stats_kernel, members, rows_side), out_s...  3.31 us
    pallas_call x3, Pallas kernels, update(): pl.pallas_call(functools.partial(update_kernel, distances, fresh), out_sh...  3 us
    pallas_call x1, Pallas kernels, stage(): pl.pallas_call(functools.partial(stage_kernel, n), out_shape=[jax.ShapeDt...  2.82 us
    pallas_call x1, Pallas kernels, precondition(): pl.pallas_call(functools.partial(precond_kernel, members), out_shape=[jax...  1.72 us
    pallas_call x1, Pallas kernels, route(): pl.pallas_call(route_kernel, out_shape=[jax.ShapeDtypeStruct((rows, width...  1.42 us
  transfers between devices with their start and end apart: 25, of which 9 were waited for; matrix products, arithmetic and copies ran while one was open for 0% of the time, Pallas kernels for 19%

profile of v1, /device:TPU:0, one launch (start us, length us, event | category | flops | bytes accessed | tf_op | source)
XLA Modules:
  0.0 53.2 jit_solution(6777358059063433832)
XLA Ops:
  0.6 3.0 %collective-permute-start.13 = (bf16[256,1024]{1,0:T(8,128)(2,1)}, bf16[256,1024]{1,0:T(8,128)(2,1)S(1)}, u32[]{:S(2)}, u32[]{:S(2)}) collective-permute-start(bf16[256,1024]{1,0:T(8,128)(2,1)} %bitcast.23), channel_id=1, source_target_pairs={{0,2},{1,3},{2,0},{3,1},{4,6},{5,7},{6,4},{7,5},{8,10},{9,11},{10,... | collective-permute-start | bytes 1572872 | tf_op jit(solution)/shard_map/ppermute | solution.py:27
  3.7 1.4 %route.1 = (bf16[32,1024]{1,0:T(8,128)(2,1)S(1)}, bf16[32,1024]{1,0:T(8,128)(2,1)S(1)}, bf16[32,1024]{1,0:T(8,128)(2,1)S(1)}, bf16[32,1024]{1,0:T(8,128)(2,1)S(1...) custom-call(s32[8]{0:T(128)} %owner_ref.3, ...), custom_call_target="tpu_custom_call" | custom-call | bytes 1572864 | tf_op jit(solution)/shard_map/route/pallas_call | solution.py:64
  5.1 2.6 %collective-permute-start = (bf16[32,1024]{1,0:T(8,128)(2,1)S(1)}, bf16[32,1024]{1,0:T(8,128)(2,1)S(1)}, u32[]{:S(2)}, u32[]{:S(2)}) collective-permute-start(bf16[32,1024]{1,0:T(8,128)(2,1)S(1)} %get-tuple-element.39), channel_id=1, source_target_pairs={{0,16},{4,20},{8,24},{12,28},{16,0},{20,4},{24,8},{28,12},{1,17},{... | collective-permute-start | bytes 196616 | tf_op jit(solution)/shard_map/ppermute | solution.py:27
  7.7 1.5 %collective-permute-start.2 = (bf16[32,1024]{1,0:T(8,128)(2,1)S(1)}, bf16[32,1024]{1,0:T(8,128)(2,1)S(1)}, u32[]{:S(2)}, u32[]{:S(2)}) collective-permute-start(bf16[32,1024]{1,0:T(8,128)(2,1)S(1)} %get-tuple-element.41), channel_id=1, source_target_pairs={{0,4},{4,0},{8,12},{12,8},{16,20},{20,16},{24,28},{28,24},{1,5},{5... | collective-permute-start | bytes 196616 | tf_op jit(solution)/shard_map/ppermute | solution.py:27
  9.2 1.5 %collective-permute-start.3 = (bf16[32,1024]{1,0:T(8,128)(2,1)S(1)}, bf16[32,1024]{1,0:T(8,128)(2,1)S(1)}, u32[]{:S(2)}, u32[]{:S(2)}) collective-permute-start(bf16[32,1024]{1,0:T(8,128)(2,1)S(1)} %get-tuple-element.43), channel_id=1, source_target_pairs={{0,12},{4,8},{8,4},{12,0},{16,28},{20,24},{24,20},{28,16},{1,13},{... | collective-permute-start | bytes 196616 | tf_op jit(solution)/shard_map/ppermute | solution.py:27
  10.7 1.3 %collective-permute-start.1 = (bf16[32,1024]{1,0:T(8,128)(2,1)S(1)}, bf16[32,1024]{1,0:T(8,128)(2,1)S(1)}, u32[]{:S(2)}, u32[]{:S(2)}) collective-permute-start(bf16[32,1024]{1,0:T(8,128)(2,1)S(1)} %get-tuple-element.40), channel_id=1, source_target_pairs={{0,20},{4,16},{8,28},{12,24},{16,4},{20,0},{24,12},{28,8},{1,21},{... | collective-permute-start | bytes 196616 | tf_op jit(solution)/shard_map/ppermute | solution.py:27
  12.0 2.8 %collective-permute-start.6 = (bf16[32,1024]{1,0:T(8,128)(2,1)S(1)}, bf16[32,1024]{1,0:T(8,128)(2,1)S(1)}, u32[]{:S(2)}, u32[]{:S(2)}) collective-permute-start(bf16[32,1024]{1,0:T(8,128)(2,1)S(1)} %after.5), channel_id=1, source_target_pairs={{0,24},{4,28},{8,16},{12,20},{16,8},{20,12},{24,0},{28,4},{1,25},{... | collective-permute-start | bytes 196616 | tf_op jit(solution)/shard_map/ppermute | solution.py:27
  14.8 2.1 %collective-permute-start.5 = (bf16[32,1024]{1,0:T(8,128)(2,1)S(1)}, bf16[32,1024]{1,0:T(8,128)(2,1)S(1)}, u32[]{:S(2)}, u32[]{:S(2)}) collective-permute-start(bf16[32,1024]{1,0:T(8,128)(2,1)S(1)} %after.4), channel_id=1, source_target_pairs={{0,28},{4,24},{8,20},{12,16},{16,12},{20,8},{24,4},{28,0},{1,29},{... | collective-permute-start | bytes 196616 | tf_op jit(solution)/shard_map/ppermute | solution.py:27
  16.9 2.6 %collective-permute-done.1.refs_1_ = bf16[32,1024]{1,0:T(8,128)(2,1)S(1)} collective-permute-done((bf16[32,1024]{1,0:T(8,128)(2,1)S(1)}, bf16[32,1024]{1,0:T(8,128)(2,1)S(1)}, u32[]{:S(2)}, u32[]{:S(2)}) %collective-permute-start.1) | collective-permute-done | bytes 65568 | tf_op jit(solution)/shard_map/ppermute | solution.py:27
  20.1 1.8 %collective-permute-done.5.refs_2_ = bf16[32,1024]{1,0:T(8,128)(2,1)S(1)} collective-permute-done((bf16[32,1024]{1,0:T(8,128)(2,1)S(1)}, bf16[32,1024]{1,0:T(8,128)(2,1)S(1)}, u32[]{:S(2)}, u32[]{:S(2)}) %collective-permute-start.5) | collective-permute-done | bytes 65568 | tf_op jit(solution)/shard_map/ppermute | solution.py:27
  22.5 2.8 %stage.1 = (bf16[256,1024]{1,0:T(8,128)(2,1)S(1)}, bf16[256,1024]{1,0:T(8,128)(2,1)S(1)}, f32[256,1024]{1,0:T(8,128)S(1)}, f32[256,1024]{1,0:T(8,128)S(1)}, f32[...) custom-call(s32[8]{0:T(128)} %owner_ref.3, f32[32,8192]{1,0:T(8,128)} %bitcast.17, ...), custom_call_target="tpu_custom_call" | custom-call | bytes 10485760 | tf_op jit(solution)/shard_map/stage/pallas_call | solution.py:286
  26.0 1.4 %collective-permute-done.8.first_ref = bf16[128,1024]{1,0:T(8,128)(2,1)S(1)} collective-permute-done((bf16[128,1024]{1,0:T(8,128)(2,1)S(1)}, bf16[128,1024]{1,0:T(8,128)(2,1)S(1)}, u32[]{:S(2)}, u32[]{:S(2)}) %collective-permute-start.8) | collective-permute-done | bytes 262176 | tf_op jit(solution)/shard_map/ppermute | solution.py:27
  27.5 2.8 %collective-permute-done.9.second_ref = bf16[128,1024]{1,0:T(8,128)(2,1)S(1)} collective-permute-done((bf16[128,1024]{1,0:T(8,128)(2,1)S(1)}, bf16[128,1024]{1,0:T(8,128)(2,1)S(1)}, u32[]{:S(2)}, u32[]{:S(2)}) %collective-permute-start.9) | collective-permute-done | bytes 262176 | tf_op jit(solution)/shard_map/ppermute | solution.py:27
  30.3 1.5 %collective-permute-done.11.second_ref = bf16[128,1024]{1,0:T(8,128)(2,1)S(1)} collective-permute-done((bf16[128,1024]{1,0:T(8,128)(2,1)S(1)}, bf16[128,1024]{1,0:T(8,128)(2,1)S(1)}, u32[]{:S(2)}, u32[]{:S(2)}) %collective-permute-start.11) | collective-permute-done | bytes 262176 | tf_op jit(solution)/shard_map/ppermute | solution.py:27
  31.9 1.7 %precondition.1 = (f32[256,1024]{1,0:T(8,128)S(1)}, f32[8,128]{1,0:T(8,128)S(1)}) custom-call(bf16[256,1024]{1,0:T(8,128)(2,1)S(1)} %get-tuple-element.50.left_ref, bf16[256,1024]{1,0:T(8,128)(2,1)S(1)} %join.3.refs_0_, bf16[256,1024]{1,0:T(8,128)(2,1)S(1)} %collective-permute-done.7.refs_1_, bf16[256,1024]{1,0:T(8,128)(2,1)S(1)} %join.4.refs_2_, ...), custom_call_target="tpu_custom_call" | custom-call | flops 1073741824 | bytes 5242880 | tf_op jit(solution)/shard_map/precondition/pallas_call | solution.py:169
  33.9 1.5 %collective-permute-start.16 = (f32[8,128]{1,0:T(8,128)S(1)}, f32[8,128]{1,0:T(8,128)S(1)}, u32[]{:S(2)}, u32[]{:S(2)}) collective-permute-start(f32[8,128]{1,0:T(8,128)S(1)} %get-tuple-element.53.refs_0_), channel_id=1, source_target_pairs={{0,2},{1,3},{2,0},{3,1},{4,6},{5,7},{6,4},{7,5},{8,10},{9,11},{10,... | collective-permute-start | bytes 12296 | tf_op jit(solution)/shard_map/ppermute | solution.py:27
  35.5 1.7 %left_statistic.1.refs_4_ = f32[256,1024]{1,0:T(8,128)} custom-call(f32[256,1024]{1,0:T(8,128)S(1)} %get-tuple-element.54.old_ref, bf16[256,1024]{1,0:T(8,128)(2,1)S(1)} %join.3.refs_0_, bf16[256,1024]{1,0:T(8,128)(2,1)S(1)} %collective-permute-done.7.refs_1_, bf16[256,1024]{1,0:T(8,128)(2,1)S(1)} %join.4.refs_2_, bf16[256,1024]{1,0:T(8,128)(2,1)S(1)} %join.5.refs_3_), custom_call_target="tpu_custom_call" | custom-call | flops 536870912 | bytes 4194304 | tf_op jit(solution)/shard_map/left_statistic/pallas_call | solution.py:240
  37.7 1.6 %collective-permute-start.22 = (bf16[32,1024]{1,0:T(8,128)(2,1)S(1)}, bf16[32,1024]{1,0:T(8,128)(2,1)S(1)}, u32[]{:S(2)}, u32[]{:S(2)}) collective-permute-start(bf16[32,1024]{1,0:T(8,128)(2,1)S(1)} %get-tuple-element.59), channel_id=1, source_target_pairs={{0,16},{4,20},{8,24},{12,28},{16,0},{20,4},{24,8},{28,12},{1,17},{... | collective-permute-start | bytes 196616 | tf_op jit(solution)/shard_map/ppermute | solution.py:27
  40.2 1.9 %collective-permute-start.24 = (bf16[32,1024]{1,0:T(8,128)(2,1)S(1)}, bf16[32,1024]{1,0:T(8,128)(2,1)S(1)}, u32[]{:S(2)}, u32[]{:S(2)}) collective-permute-start(bf16[32,1024]{1,0:T(8,128)(2,1)S(1)} %get-tuple-element.61), channel_id=1, source_target_pairs={{0,20},{4,16},{8,28},{12,24},{16,4},{20,0},{24,12},{28,8},{1,21},{... | collective-permute-start | bytes 196616 | tf_op jit(solution)/shard_map/ppermute | solution.py:27
  42.1 2.2 %collective-permute-start.20 = (bf16[32,1024]{1,0:T(8,128)(2,1)S(1)}, bf16[32,1024]{1,0:T(8,128)(2,1)S(1)}, u32[]{:S(2)}, u32[]{:S(2)}) collective-permute-start(bf16[32,1024]{1,0:T(8,128)(2,1)S(1)} %get-tuple-element.57), channel_id=1, source_target_pairs={{0,24},{4,28},{8,16},{12,20},{16,8},{20,12},{24,0},{28,4},{1,25},{... | collective-permute-start | bytes 196616 | tf_op jit(solution)/shard_map/ppermute | solution.py:27
  45.1 1.7 %collective-permute-start.18 = (bf16[32,1024]{1,0:T(8,128)(2,1)S(1)}, bf16[32,1024]{1,0:T(8,128)(2,1)S(1)}, u32[]{:S(2)}, u32[]{:S(2)}) collective-permute-start(bf16[32,1024]{1,0:T(8,128)(2,1)S(1)} %get-tuple-element.55), channel_id=1, source_target_pairs={{0,28},{4,24},{8,20},{12,16},{16,12},{20,8},{24,4},{28,0},{1,29},{... | collective-permute-start | bytes 196616 | tf_op jit(solution)/shard_map/ppermute | solution.py:27
  46.8 1.2 %collective-permute-start.19 = (bf16[32,1024]{1,0:T(8,128)(2,1)S(1)}, bf16[32,1024]{1,0:T(8,128)(2,1)S(1)}, u32[]{:S(2)}, u32[]{:S(2)}) collective-permute-start(bf16[32,1024]{1,0:T(8,128)(2,1)S(1)} %get-tuple-element.56), channel_id=1, source_target_pairs={{0,8},{4,12},{8,0},{12,4},{16,24},{20,28},{24,16},{28,20},{1,9},{5... | collective-permute-start | bytes 196616 | tf_op jit(solution)/shard_map/ppermute | solution.py:27
  48.0 1.7 %right_statistic.1 = f32[256,1024]{1,0:T(8,128)} custom-call(f32[256,1024]{1,0:T(8,128)S(1)} %get-tuple-element.72.old_ref, bf16[256,1024]{1,0:T(8,128)(2,1)S(1)} %join.3.refs_0_, bf16[256,1024]{1,0:T(8,128)(2,1)S(1)} %collective-permute-done.7.refs_1_, bf16[256,1024]{1,0:T(8,128)(2,1)S(1)} %join.4.refs_2_, bf16[256,1024]{1,0:T(8,128)(2,1)S(1)} %join.5.refs_3_), custom_call_target="tpu_custom_call" | custom-call | flops 536870912 | bytes 4194304 | tf_op jit(solution)/shard_map/right_statistic/pallas_call | solution.py:240
  49.7 1.2 %update.3 = (f32[32,8192]{1,0:T(8,128)}, f32[32,8192]{1,0:T(8,128)}, bf16[32,8192]{1,0:T(8,128)(2,1)}) custom-call(s32[8,128]{1,0:T(8,128)S(1)} %get-tuple-element.47.block_ref, f32[8,32,1024]{2,1,0:T(8,128)S(1)} %get-tuple-element.48.refs_0_.z_ref, f32[8,32,1024]{2,1,0:T(8,128)S(1)} %get-tuple-element.49.x_ref, ...), custom_call_target="tpu_custom_call" | custom-call | flops 1048576 | bytes 2621440 | tf_op jit(solution)/shard_map/update/pallas_call | solution.py:334
  (43 shorter events, 7.0 us)
Async XLA Ops:
  0.6 25.3 %collective-permute-start.13 = (bf16[256,1024]{1,0:T(8,128)(2,1)}, bf16[256,1024]{1,0:T(8,128)(2,1)S(1)}, u32[]{:S(2)}, u32[]{:S(2)}) collective-permute-start(bf16[256,1024]{1,0:T(8,128)(2,1)} %bitcast.23), channel_id=1, source_target_pairs={{0,2},{1,3},{2,0},{3,1},{4,6},{5,7},{6,4},{7,5},{8,10},{9,11},{10,... | collective-permute-start | bytes 1572872 | tf_op jit(solution)/shard_map/ppermute | solution.py:27
  5.1 7.0 %collective-permute-start = (bf16[32,1024]{1,0:T(8,128)(2,1)S(1)}, bf16[32,1024]{1,0:T(8,128)(2,1)S(1)}, u32[]{:S(2)}, u32[]{:S(2)}) collective-permute-start(bf16[32,1024]{1,0:T(8,128)(2,1)S(1)} %get-tuple-element.39), channel_id=1, source_target_pairs={{0,16},{4,20},{8,24},{12,28},{16,0},{20,4},{24,8},{28,12},{1,17},{... | collective-permute-start | bytes 196616 | tf_op jit(solution)/shard_map/ppermute | solution.py:27
  7.7 7.1 %collective-permute-start.2 = (bf16[32,1024]{1,0:T(8,128)(2,1)S(1)}, bf16[32,1024]{1,0:T(8,128)(2,1)S(1)}, u32[]{:S(2)}, u32[]{:S(2)}) collective-permute-start(bf16[32,1024]{1,0:T(8,128)(2,1)S(1)} %get-tuple-element.41), channel_id=1, source_target_pairs={{0,4},{4,0},{8,12},{12,8},{16,20},{20,16},{24,28},{28,24},{1,5},{5... | collective-permute-start | bytes 196616 | tf_op jit(solution)/shard_map/ppermute | solution.py:27
  9.2 7.7 %collective-permute-start.3 = (bf16[32,1024]{1,0:T(8,128)(2,1)S(1)}, bf16[32,1024]{1,0:T(8,128)(2,1)S(1)}, u32[]{:S(2)}, u32[]{:S(2)}) collective-permute-start(bf16[32,1024]{1,0:T(8,128)(2,1)S(1)} %get-tuple-element.43), channel_id=1, source_target_pairs={{0,12},{4,8},{8,4},{12,0},{16,28},{20,24},{24,20},{28,16},{1,13},{... | collective-permute-start | bytes 196616 | tf_op jit(solution)/shard_map/ppermute | solution.py:27
  10.7 8.7 %collective-permute-start.1 = (bf16[32,1024]{1,0:T(8,128)(2,1)S(1)}, bf16[32,1024]{1,0:T(8,128)(2,1)S(1)}, u32[]{:S(2)}, u32[]{:S(2)}) collective-permute-start(bf16[32,1024]{1,0:T(8,128)(2,1)S(1)} %get-tuple-element.40), channel_id=1, source_target_pairs={{0,20},{4,16},{8,28},{12,24},{16,4},{20,0},{24,12},{28,8},{1,21},{... | collective-permute-start | bytes 196616 | tf_op jit(solution)/shard_map/ppermute | solution.py:27
  12.0 8.0 %collective-permute-start.6 = (bf16[32,1024]{1,0:T(8,128)(2,1)S(1)}, bf16[32,1024]{1,0:T(8,128)(2,1)S(1)}, u32[]{:S(2)}, u32[]{:S(2)}) collective-permute-start(bf16[32,1024]{1,0:T(8,128)(2,1)S(1)} %after.5), channel_id=1, source_target_pairs={{0,24},{4,28},{8,16},{12,20},{16,8},{20,12},{24,0},{28,4},{1,25},{... | collective-permute-start | bytes 196616 | tf_op jit(solution)/shard_map/ppermute | solution.py:27
  14.8 7.1 %collective-permute-start.5 = (bf16[32,1024]{1,0:T(8,128)(2,1)S(1)}, bf16[32,1024]{1,0:T(8,128)(2,1)S(1)}, u32[]{:S(2)}, u32[]{:S(2)}) collective-permute-start(bf16[32,1024]{1,0:T(8,128)(2,1)S(1)} %after.4), channel_id=1, source_target_pairs={{0,28},{4,24},{8,20},{12,16},{16,12},{20,8},{24,4},{28,0},{1,29},{... | collective-permute-start | bytes 196616 | tf_op jit(solution)/shard_map/ppermute | solution.py:27
  16.9 5.0 %collective-permute-start.4 = (bf16[32,1024]{1,0:T(8,128)(2,1)S(1)}, bf16[32,1024]{1,0:T(8,128)(2,1)S(1)}, u32[]{:S(2)}, u32[]{:S(2)}) collective-permute-start(bf16[32,1024]{1,0:T(8,128)(2,1)S(1)} %after.3), channel_id=1, source_target_pairs={{0,8},{4,12},{8,0},{12,4},{16,24},{20,28},{24,16},{28,20},{1,9},{5... | collective-permute-start | bytes 196616 | tf_op jit(solution)/shard_map/ppermute | solution.py:27
  19.5 7.9 %collective-permute-start.8 = (bf16[128,1024]{1,0:T(8,128)(2,1)S(1)}, bf16[128,1024]{1,0:T(8,128)(2,1)S(1)}, u32[]{:S(2)}, u32[]{:S(2)}) collective-permute-start(bf16[128,1024]{1,0:T(8,128)(2,1)S(1)} %half.2.refs_4_.first_ref), channel_id=1, source_target_pairs={{0,2},{1,3},{2,0},{3,1},{4,6},{5,7},{6,4},{7,5},{8,10},{9,11},{10,... | collective-permute-start | bytes 786440 | tf_op jit(solution)/shard_map/ppermute | solution.py:27
  21.9 8.3 %collective-permute-start.9 = (bf16[128,1024]{1,0:T(8,128)(2,1)S(1)}, bf16[128,1024]{1,0:T(8,128)(2,1)S(1)}, u32[]{:S(2)}, u32[]{:S(2)}) collective-permute-start(bf16[128,1024]{1,0:T(8,128)(2,1)S(1)} %half.3.refs_5_.second_ref), channel_id=1, source_target_pairs={{0,2},{1,3},{2,0},{3,1},{4,6},{5,7},{6,4},{7,5},{8,10},{9,11},{10,... | collective-permute-start | bytes 786440 | tf_op jit(solution)/shard_map/ppermute | solution.py:27
  25.4 6.5 %collective-permute-start.12 = (bf16[256,1024]{1,0:T(8,128)(2,1)S(1)}, bf16[256,1024]{1,0:T(8,128)(2,1)S(1)}, u32[]{:S(2)}, u32[]{:S(2)}) collective-permute-start(bf16[256,1024]{1,0:T(8,128)(2,1)S(1)} %get-tuple-element.51.refs_4_), channel_id=1, source_target_pairs={{0,1},{1,0},{2,3},{3,2},{4,5},{5,4},{6,7},{7,6},{8,9},{9,8},{10,11... | collective-permute-start | bytes 1572872 | tf_op jit(solution)/shard_map/ppermute | solution.py:27
  25.5 6.4 %collective-permute-start.7 = (bf16[256,1024]{1,0:T(8,128)(2,1)S(1)}, bf16[256,1024]{1,0:T(8,128)(2,1)S(1)}, u32[]{:S(2)}, u32[]{:S(2)}) collective-permute-start(bf16[256,1024]{1,0:T(8,128)(2,1)S(1)} %join.3.refs_0_), channel_id=1, source_target_pairs={{0,1},{1,0},{2,3},{3,2},{4,5},{5,4},{6,7},{7,6},{8,9},{9,8},{10,11... | collective-permute-start | bytes 1572872 | tf_op jit(solution)/shard_map/ppermute | solution.py:27
  26.0 5.9 %collective-permute-start.14 = (bf16[256,1024]{1,0:T(8,128)(2,1)S(1)}, bf16[256,1024]{1,0:T(8,128)(2,1)S(1)}, u32[]{:S(2)}, u32[]{:S(2)}) collective-permute-start(bf16[256,1024]{1,0:T(8,128)(2,1)S(1)} %collective-permute-done.13.refs_6_), channel_id=1, source_target_pairs={{0,1},{1,0},{2,3},{3,2},{4,5},{5,4},{6,7},{7,6},{8,9},{9,8},{10,11... | collective-permute-start | bytes 1572872 | tf_op jit(solution)/shard_map/ppermute | solution.py:27
  27.4 2.9 %collective-permute-start.10 = (bf16[128,1024]{1,0:T(8,128)(2,1)S(1)}, bf16[128,1024]{1,0:T(8,128)(2,1)S(1)}, u32[]{:S(2)}, u32[]{:S(2)}) collective-permute-start(bf16[128,1024]{1,0:T(8,128)(2,1)S(1)} %collective-permute-done.8.first_ref), channel_id=1, source_target_pairs={{0,1},{1,0},{2,3},{3,2},{4,5},{5,4},{6,7},{7,6},{8,9},{9,8},{10,11... | collective-permute-start | bytes 786440 | tf_op jit(solution)/shard_map/ppermute | solution.py:27
  33.6 3.6 %collective-permute-start.17 = (f32[8,128]{1,0:T(8,128)S(1)}, f32[8,128]{1,0:T(8,128)S(1)}, u32[]{:S(2)}, u32[]{:S(2)}) collective-permute-start(f32[8,128]{1,0:T(8,128)S(1)} %get-tuple-element.53.refs_0_), channel_id=1, source_target_pairs={{0,3},{1,2},{2,1},{3,0},{4,7},{5,6},{6,5},{7,4},{8,11},{9,10},{10,... | collective-permute-start | bytes 12296 | tf_op jit(solution)/shard_map/ppermute | solution.py:27
  33.9 3.6 %collective-permute-start.16 = (f32[8,128]{1,0:T(8,128)S(1)}, f32[8,128]{1,0:T(8,128)S(1)}, u32[]{:S(2)}, u32[]{:S(2)}) collective-permute-start(f32[8,128]{1,0:T(8,128)S(1)} %get-tuple-element.53.refs_0_), channel_id=1, source_target_pairs={{0,2},{1,3},{2,0},{3,1},{4,6},{5,7},{6,4},{7,5},{8,10},{9,11},{10,... | collective-permute-start | bytes 12296 | tf_op jit(solution)/shard_map/ppermute | solution.py:27
  35.5 2.1 %collective-permute-start.15 = (f32[8,128]{1,0:T(8,128)S(1)}, f32[8,128]{1,0:T(8,128)S(1)}, u32[]{:S(2)}, u32[]{:S(2)}) collective-permute-start(f32[8,128]{1,0:T(8,128)S(1)} %get-tuple-element.53.refs_0_), channel_id=1, source_target_pairs={{0,1},{1,0},{2,3},{3,2},{4,5},{5,4},{6,7},{7,6},{8,9},{9,8},{10,11... | collective-permute-start | bytes 12296 | tf_op jit(solution)/shard_map/ppermute | solution.py:27
  37.7 7.5 %collective-permute-start.22 = (bf16[32,1024]{1,0:T(8,128)(2,1)S(1)}, bf16[32,1024]{1,0:T(8,128)(2,1)S(1)}, u32[]{:S(2)}, u32[]{:S(2)}) collective-permute-start(bf16[32,1024]{1,0:T(8,128)(2,1)S(1)} %get-tuple-element.59), channel_id=1, source_target_pairs={{0,16},{4,20},{8,24},{12,28},{16,0},{20,4},{24,8},{28,12},{1,17},{... | collective-permute-start | bytes 196616 | tf_op jit(solution)/shard_map/ppermute | solution.py:27
  39.3 7.6 %collective-permute-start.23 = (bf16[32,1024]{1,0:T(8,128)(2,1)S(1)}, bf16[32,1024]{1,0:T(8,128)(2,1)S(1)}, u32[]{:S(2)}, u32[]{:S(2)}) collective-permute-start(bf16[32,1024]{1,0:T(8,128)(2,1)S(1)} %get-tuple-element.60), channel_id=1, source_target_pairs={{0,4},{4,0},{8,12},{12,8},{16,20},{20,16},{24,28},{28,24},{1,5},{5... | collective-permute-start | bytes 196616 | tf_op jit(solution)/shard_map/ppermute | solution.py:27
  40.2 9.4 %collective-permute-start.24 = (bf16[32,1024]{1,0:T(8,128)(2,1)S(1)}, bf16[32,1024]{1,0:T(8,128)(2,1)S(1)}, u32[]{:S(2)}, u32[]{:S(2)}) collective-permute-start(bf16[32,1024]{1,0:T(8,128)(2,1)S(1)} %get-tuple-element.61), channel_id=1, source_target_pairs={{0,20},{4,16},{8,28},{12,24},{16,4},{20,0},{24,12},{28,8},{1,21},{... | collective-permute-start | bytes 196616 | tf_op jit(solution)/shard_map/ppermute | solution.py:27
  42.1 8.7 %collective-permute-start.20 = (bf16[32,1024]{1,0:T(8,128)(2,1)S(1)}, bf16[32,1024]{1,0:T(8,128)(2,1)S(1)}, u32[]{:S(2)}, u32[]{:S(2)}) collective-permute-start(bf16[32,1024]{1,0:T(8,128)(2,1)S(1)} %get-tuple-element.57), channel_id=1, source_target_pairs={{0,24},{4,28},{8,16},{12,20},{16,8},{20,12},{24,0},{28,4},{1,25},{... | collective-permute-start | bytes 196616 | tf_op jit(solution)/shard_map/ppermute | solution.py:27
  44.3 7.0 %collective-permute-start.21 = (bf16[32,1024]{1,0:T(8,128)(2,1)S(1)}, bf16[32,1024]{1,0:T(8,128)(2,1)S(1)}, u32[]{:S(2)}, u32[]{:S(2)}) collective-permute-start(bf16[32,1024]{1,0:T(8,128)(2,1)S(1)} %get-tuple-element.58), channel_id=1, source_target_pairs={{0,12},{4,8},{8,4},{12,0},{16,28},{20,24},{24,20},{28,16},{1,13},{... | collective-permute-start | bytes 196616 | tf_op jit(solution)/shard_map/ppermute | solution.py:27
  45.1 7.1 %collective-permute-start.18 = (bf16[32,1024]{1,0:T(8,128)(2,1)S(1)}, bf16[32,1024]{1,0:T(8,128)(2,1)S(1)}, u32[]{:S(2)}, u32[]{:S(2)}) collective-permute-start(bf16[32,1024]{1,0:T(8,128)(2,1)S(1)} %get-tuple-element.55), channel_id=1, source_target_pairs={{0,28},{4,24},{8,20},{12,16},{16,12},{20,8},{24,4},{28,0},{1,29},{... | collective-permute-start | bytes 196616 | tf_op jit(solution)/shard_map/ppermute | solution.py:27
  46.8 5.4 %collective-permute-start.19 = (bf16[32,1024]{1,0:T(8,128)(2,1)S(1)}, bf16[32,1024]{1,0:T(8,128)(2,1)S(1)}, u32[]{:S(2)}, u32[]{:S(2)}) collective-permute-start(bf16[32,1024]{1,0:T(8,128)(2,1)S(1)} %get-tuple-element.56), channel_id=1, source_target_pairs={{0,8},{4,12},{8,0},{12,4},{16,24},{20,28},{24,16},{28,20},{1,9},{5... | collective-permute-start | bytes 196616 | tf_op jit(solution)/shard_map/ppermute | solution.py:27
  (1 other events, 1.5 us)

commit v2 on v1

--- a/solution.py
+++ b/solution.py
@@ -403,7 +403,7 @@
     for d in (4, 1, 5, 6, 7, 3, 2):
         back[d] = send(piece[d], d)
     new = None
-    for distances in ((4, 1, 5, 0), (6, 3), (7, 2)):
+    for distances in ((4, 1, 5, 6, 0), (7, 3, 2)):
         new = update(block, z, x, back, distances, new)
     return (*new, left_new, statistic(stat_right, blocks, False))
 

time: 53.3 us -> 53.9 us (1.011)
  starting transfers between devices: 28.3 us -> 29.8 us
  Pallas kernels: 12.6 us -> 11.9 us
    ppermute x25, starting transfers between devices: 28.3 us -> 29.8 us  [swap(): return lax.ppermute(x, axis, [(i, i ^ bit) for i in range(size)])]
    pallas_call x3 -> x2, Pallas kernels: 3 us -> 2.36 us  [update(): pl.pallas_call(functools.partial(update_kernel, distances, fresh), out_sh...]
  transfers between devices with their start and end apart: 25 -> 25, of which waited for: 9 -> 8; matrix products, arithmetic and copies ran while one was open for 0% -> 0% of each run, Pallas kernels for 19% -> 17%
where the time goes in v2:
time: 53.9 us; the launch traced here: 53.7 us
  starting transfers between devices  29.8 us (55%)
  Pallas kernels  11.9 us (22%)
  waiting for transfers between devices  11.2 us (21%)
  between operations  0.81 us (2%)
    ppermute x25, starting transfers between devices, swap(): return lax.ppermute(x, axis, [(i, i ^ bit) for i in range(size)])  29.8 us
    ppermute x25, waiting for transfers between devices, swap(): return lax.ppermute(x, axis, [(i, i ^ bit) for i in range(size)])  11.2 us
    pallas_call x2, Pallas kernels, statistic(): pl.pallas_call(functools.partial(stats_kernel, members, rows_side), out_s...  3.3 us
    pallas_call x1, Pallas kernels, stage(): pl.pallas_call(functools.partial(stage_kernel, n), out_shape=[jax.ShapeDt...  2.82 us
    pallas_call x2, Pallas kernels, update(): pl.pallas_call(functools.partial(update_kernel, distances, fresh), out_sh...  2.36 us
    pallas_call x1, Pallas kernels, precondition(): pl.pallas_call(functools.partial(precond_kernel, members), out_shape=[jax...  1.71 us
    pallas_call x1, Pallas kernels, route(): pl.pallas_call(route_kernel, out_shape=[jax.ShapeDtypeStruct((rows, width...  1.38 us
  transfers between devices with their start and end apart: 25, of which 8 were waited for; matrix products, arithmetic and copies ran while one was open for 0% of the time, Pallas kernels for 17%

profile of v2, /device:TPU:0, one launch (start us, length us, event | category | flops | bytes accessed | tf_op | source)
XLA Modules:
  0.0 53.7 jit_solution(15624223478225365428)
XLA Ops:
  0.6 3.0 %collective-permute-start.13 = (bf16[256,1024]{1,0:T(8,128)(2,1)}, bf16[256,1024]{1,0:T(8,128)(2,1)S(1)}, u32[]{:S(2)}, u32[]{:S(2)}) collective-permute-start(bf16[256,1024]{1,0:T(8,128)(2,1)} %bitcast.22), channel_id=1, source_target_pairs={{0,2},{1,3},{2,0},{3,1},{4,6},{5,7},{6,4},{7,5},{8,10},{9,11},{10,... | collective-permute-start | bytes 1572872 | tf_op jit(solution)/shard_map/ppermute | solution.py:27
  3.7 1.4 %route.1 = (bf16[32,1024]{1,0:T(8,128)(2,1)S(1)}, bf16[32,1024]{1,0:T(8,128)(2,1)S(1)}, bf16[32,1024]{1,0:T(8,128)(2,1)S(1)}, bf16[32,1024]{1,0:T(8,128)(2,1)S(1...) custom-call(s32[8]{0:T(128)} %owner_ref.3, ...), custom_call_target="tpu_custom_call" | custom-call | bytes 1572864 | tf_op jit(solution)/shard_map/route/pallas_call | solution.py:64
  5.1 2.7 %collective-permute-start = (bf16[32,1024]{1,0:T(8,128)(2,1)S(1)}, bf16[32,1024]{1,0:T(8,128)(2,1)S(1)}, u32[]{:S(2)}, u32[]{:S(2)}) collective-permute-start(bf16[32,1024]{1,0:T(8,128)(2,1)S(1)} %get-tuple-element.36), channel_id=1, source_target_pairs={{0,16},{4,20},{8,24},{12,28},{16,0},{20,4},{24,8},{28,12},{1,17},{... | collective-permute-start | bytes 196616 | tf_op jit(solution)/shard_map/ppermute | solution.py:27
  7.7 1.5 %collective-permute-start.2 = (bf16[32,1024]{1,0:T(8,128)(2,1)S(1)}, bf16[32,1024]{1,0:T(8,128)(2,1)S(1)}, u32[]{:S(2)}, u32[]{:S(2)}) collective-permute-start(bf16[32,1024]{1,0:T(8,128)(2,1)S(1)} %get-tuple-element.38), channel_id=1, source_target_pairs={{0,4},{4,0},{8,12},{12,8},{16,20},{20,16},{24,28},{28,24},{1,5},{5... | collective-permute-start | bytes 196616 | tf_op jit(solution)/shard_map/ppermute | solution.py:27
  9.2 1.6 %collective-permute-start.3 = (bf16[32,1024]{1,0:T(8,128)(2,1)S(1)}, bf16[32,1024]{1,0:T(8,128)(2,1)S(1)}, u32[]{:S(2)}, u32[]{:S(2)}) collective-permute-start(bf16[32,1024]{1,0:T(8,128)(2,1)S(1)} %get-tuple-element.40), channel_id=1, source_target_pairs={{0,12},{4,8},{8,4},{12,0},{16,28},{20,24},{24,20},{28,16},{1,13},{... | collective-permute-start | bytes 196616 | tf_op jit(solution)/shard_map/ppermute | solution.py:27
  10.8 1.2 %collective-permute-start.1 = (bf16[32,1024]{1,0:T(8,128)(2,1)S(1)}, bf16[32,1024]{1,0:T(8,128)(2,1)S(1)}, u32[]{:S(2)}, u32[]{:S(2)}) collective-permute-start(bf16[32,1024]{1,0:T(8,128)(2,1)S(1)} %get-tuple-element.37), channel_id=1, source_target_pairs={{0,20},{4,16},{8,28},{12,24},{16,4},{20,0},{24,12},{28,8},{1,21},{... | collective-permute-start | bytes 196616 | tf_op jit(solution)/shard_map/ppermute | solution.py:27
  12.0 2.9 %collective-permute-start.6 = (bf16[32,1024]{1,0:T(8,128)(2,1)S(1)}, bf16[32,1024]{1,0:T(8,128)(2,1)S(1)}, u32[]{:S(2)}, u32[]{:S(2)}) collective-permute-start(bf16[32,1024]{1,0:T(8,128)(2,1)S(1)} %after.5), channel_id=1, source_target_pairs={{0,24},{4,28},{8,16},{12,20},{16,8},{20,12},{24,0},{28,4},{1,25},{... | collective-permute-start | bytes 196616 | tf_op jit(solution)/shard_map/ppermute | solution.py:27
  14.9 2.0 %collective-permute-start.5 = (bf16[32,1024]{1,0:T(8,128)(2,1)S(1)}, bf16[32,1024]{1,0:T(8,128)(2,1)S(1)}, u32[]{:S(2)}, u32[]{:S(2)}) collective-permute-start(bf16[32,1024]{1,0:T(8,128)(2,1)S(1)} %after.4), channel_id=1, source_target_pairs={{0,28},{4,24},{8,20},{12,16},{16,12},{20,8},{24,4},{28,0},{1,29},{... | collective-permute-start | bytes 196616 | tf_op jit(solution)/shard_map/ppermute | solution.py:27
  16.9 2.5 %collective-permute-done.1.refs_1_ = bf16[32,1024]{1,0:T(8,128)(2,1)S(1)} collective-permute-done((bf16[32,1024]{1,0:T(8,128)(2,1)S(1)}, bf16[32,1024]{1,0:T(8,128)(2,1)S(1)}, u32[]{:S(2)}, u32[]{:S(2)}) %collective-permute-start.1) | collective-permute-done | bytes 65568 | tf_op jit(solution)/shard_map/ppermute | solution.py:27
  20.1 1.9 %collective-permute-done.5.refs_2_ = bf16[32,1024]{1,0:T(8,128)(2,1)S(1)} collective-permute-done((bf16[32,1024]{1,0:T(8,128)(2,1)S(1)}, bf16[32,1024]{1,0:T(8,128)(2,1)S(1)}, u32[]{:S(2)}, u32[]{:S(2)}) %collective-permute-start.5) | collective-permute-done | bytes 65568 | tf_op jit(solution)/shard_map/ppermute | solution.py:27
  22.6 2.8 %stage.1 = (bf16[256,1024]{1,0:T(8,128)(2,1)S(1)}, bf16[256,1024]{1,0:T(8,128)(2,1)S(1)}, f32[256,1024]{1,0:T(8,128)S(1)}, f32[256,1024]{1,0:T(8,128)S(1)}, f32[...) custom-call(s32[8]{0:T(128)} %owner_ref.3, f32[32,8192]{1,0:T(8,128)} %bitcast.14, ...), custom_call_target="tpu_custom_call" | custom-call | bytes 10485760 | tf_op jit(solution)/shard_map/stage/pallas_call | solution.py:286
  26.1 1.3 %collective-permute-done.8.first_ref = bf16[128,1024]{1,0:T(8,128)(2,1)S(1)} collective-permute-done((bf16[128,1024]{1,0:T(8,128)(2,1)S(1)}, bf16[128,1024]{1,0:T(8,128)(2,1)S(1)}, u32[]{:S(2)}, u32[]{:S(2)}) %collective-permute-start.8) | collective-permute-done | bytes 262176 | tf_op jit(solution)/shard_map/ppermute | solution.py:27
  27.4 2.8 %collective-permute-done.9.second_ref = bf16[128,1024]{1,0:T(8,128)(2,1)S(1)} collective-permute-done((bf16[128,1024]{1,0:T(8,128)(2,1)S(1)}, bf16[128,1024]{1,0:T(8,128)(2,1)S(1)}, u32[]{:S(2)}, u32[]{:S(2)}) %collective-permute-start.9) | collective-permute-done | bytes 262176 | tf_op jit(solution)/shard_map/ppermute | solution.py:27
  30.3 1.5 %collective-permute-done.11.second_ref = bf16[128,1024]{1,0:T(8,128)(2,1)S(1)} collective-permute-done((bf16[128,1024]{1,0:T(8,128)(2,1)S(1)}, bf16[128,1024]{1,0:T(8,128)(2,1)S(1)}, u32[]{:S(2)}, u32[]{:S(2)}) %collective-permute-start.11) | collective-permute-done | bytes 262176 | tf_op jit(solution)/shard_map/ppermute | solution.py:27
  31.8 1.7 %precondition.1 = (f32[256,1024]{1,0:T(8,128)S(1)}, f32[8,128]{1,0:T(8,128)S(1)}) custom-call(bf16[256,1024]{1,0:T(8,128)(2,1)S(1)} %get-tuple-element.47.left_ref, bf16[256,1024]{1,0:T(8,128)(2,1)S(1)} %join.3.refs_0_, bf16[256,1024]{1,0:T(8,128)(2,1)S(1)} %collective-permute-done.7.refs_1_, bf16[256,1024]{1,0:T(8,128)(2,1)S(1)} %join.4.refs_2_, ...), custom_call_target="tpu_custom_call" | custom-call | flops 1073741824 | bytes 5242880 | tf_op jit(solution)/shard_map/precondition/pallas_call | solution.py:169
  33.9 1.5 %collective-permute-start.16 = (f32[8,128]{1,0:T(8,128)S(1)}, f32[8,128]{1,0:T(8,128)S(1)}, u32[]{:S(2)}, u32[]{:S(2)}) collective-permute-start(f32[8,128]{1,0:T(8,128)S(1)} %get-tuple-element.50.refs_0_), channel_id=1, source_target_pairs={{0,2},{1,3},{2,0},{3,1},{4,6},{5,7},{6,4},{7,5},{8,10},{9,11},{10,... | collective-permute-start | bytes 12296 | tf_op jit(solution)/shard_map/ppermute | solution.py:27
  35.5 1.7 %left_statistic.1.refs_4_ = f32[256,1024]{1,0:T(8,128)} custom-call(f32[256,1024]{1,0:T(8,128)S(1)} %get-tuple-element.51.old_ref, bf16[256,1024]{1,0:T(8,128)(2,1)S(1)} %join.3.refs_0_, bf16[256,1024]{1,0:T(8,128)(2,1)S(1)} %collective-permute-done.7.refs_1_, bf16[256,1024]{1,0:T(8,128)(2,1)S(1)} %join.4.refs_2_, bf16[256,1024]{1,0:T(8,128)(2,1)S(1)} %join.5.refs_3_), custom_call_target="tpu_custom_call" | custom-call | flops 536870912 | bytes 4194304 | tf_op jit(solution)/shard_map/left_statistic/pallas_call | solution.py:240
  37.6 1.7 %collective-permute-start.21 = (bf16[32,1024]{1,0:T(8,128)(2,1)S(1)}, bf16[32,1024]{1,0:T(8,128)(2,1)S(1)}, u32[]{:S(2)}, u32[]{:S(2)}) collective-permute-start(bf16[32,1024]{1,0:T(8,128)(2,1)S(1)} %get-tuple-element.55), channel_id=1, source_target_pairs={{0,16},{4,20},{8,24},{12,28},{16,0},{20,4},{24,8},{28,12},{1,17},{... | collective-permute-start | bytes 196616 | tf_op jit(solution)/shard_map/ppermute | solution.py:27
  40.3 1.7 %collective-permute-start.23 = (bf16[32,1024]{1,0:T(8,128)(2,1)S(1)}, bf16[32,1024]{1,0:T(8,128)(2,1)S(1)}, u32[]{:S(2)}, u32[]{:S(2)}) collective-permute-start(bf16[32,1024]{1,0:T(8,128)(2,1)S(1)} %get-tuple-element.57), channel_id=1, source_target_pairs={{0,20},{4,16},{8,28},{12,24},{16,4},{20,0},{24,12},{28,8},{1,21},{... | collective-permute-start | bytes 196616 | tf_op jit(solution)/shard_map/ppermute | solution.py:27
  42.1 2.2 %collective-permute-start.24 = (bf16[32,1024]{1,0:T(8,128)(2,1)S(1)}, bf16[32,1024]{1,0:T(8,128)(2,1)S(1)}, u32[]{:S(2)}, u32[]{:S(2)}) collective-permute-start(bf16[32,1024]{1,0:T(8,128)(2,1)S(1)} %get-tuple-element.58), channel_id=1, source_target_pairs={{0,24},{4,28},{8,16},{12,20},{16,8},{20,12},{24,0},{28,4},{1,25},{... | collective-permute-start | bytes 196616 | tf_op jit(solution)/shard_map/ppermute | solution.py:27
  44.3 2.5 %collective-permute-start.18 = (bf16[32,1024]{1,0:T(8,128)(2,1)S(1)}, bf16[32,1024]{1,0:T(8,128)(2,1)S(1)}, u32[]{:S(2)}, u32[]{:S(2)}) collective-permute-start(bf16[32,1024]{1,0:T(8,128)(2,1)S(1)} %get-tuple-element.52), channel_id=1, source_target_pairs={{0,28},{4,24},{8,20},{12,16},{16,12},{20,8},{24,4},{28,0},{1,29},{... | collective-permute-start | bytes 196616 | tf_op jit(solution)/shard_map/ppermute | solution.py:27
  46.8 2.0 %collective-permute-start.20 = (bf16[32,1024]{1,0:T(8,128)(2,1)S(1)}, bf16[32,1024]{1,0:T(8,128)(2,1)S(1)}, u32[]{:S(2)}, u32[]{:S(2)}) collective-permute-start(bf16[32,1024]{1,0:T(8,128)(2,1)S(1)} %get-tuple-element.54), channel_id=1, source_target_pairs={{0,8},{4,12},{8,0},{12,4},{16,24},{20,28},{24,16},{28,20},{1,9},{5... | collective-permute-start | bytes 196616 | tf_op jit(solution)/shard_map/ppermute | solution.py:27
  48.8 1.7 %right_statistic.1 = f32[256,1024]{1,0:T(8,128)} custom-call(f32[256,1024]{1,0:T(8,128)S(1)} %get-tuple-element.66.old_ref, bf16[256,1024]{1,0:T(8,128)(2,1)S(1)} %join.3.refs_0_, bf16[256,1024]{1,0:T(8,128)(2,1)S(1)} %collective-permute-done.7.refs_1_, bf16[256,1024]{1,0:T(8,128)(2,1)S(1)} %join.4.refs_2_, bf16[256,1024]{1,0:T(8,128)(2,1)S(1)} %join.5.refs_3_), custom_call_target="tpu_custom_call" | custom-call | flops 536870912 | bytes 4194304 | tf_op jit(solution)/shard_map/right_statistic/pallas_call | solution.py:240
  50.5 1.3 %update.2 = (f32[32,8192]{1,0:T(8,128)}, f32[32,8192]{1,0:T(8,128)}, bf16[32,8192]{1,0:T(8,128)(2,1)}) custom-call(s32[8,128]{1,0:T(8,128)S(1)} %get-tuple-element.44.block_ref, f32[8,32,1024]{2,1,0:T(8,128)S(1)} %get-tuple-element.45.refs_0_.z_ref, f32[8,32,1024]{2,1,0:T(8,128)S(1)} %get-tuple-element.46.x_ref, ...), custom_call_target="tpu_custom_call" | custom-call | flops 1310720 | bytes 3276800 | tf_op jit(solution)/shard_map/update/pallas_call | solution.py:334
  (42 shorter events, 5.9 us)
Async XLA Ops:
  0.6 25.4 %collective-permute-start.13 = (bf16[256,1024]{1,0:T(8,128)(2,1)}, bf16[256,1024]{1,0:T(8,128)(2,1)S(1)}, u32[]{:S(2)}, u32[]{:S(2)}) collective-permute-start(bf16[256,1024]{1,0:T(8,128)(2,1)} %bitcast.22), channel_id=1, source_target_pairs={{0,2},{1,3},{2,0},{3,1},{4,6},{5,7},{6,4},{7,5},{8,10},{9,11},{10,... | collective-permute-start | bytes 1572872 | tf_op jit(solution)/shard_map/ppermute | solution.py:27
  5.1 7.0 %collective-permute-start = (bf16[32,1024]{1,0:T(8,128)(2,1)S(1)}, bf16[32,1024]{1,0:T(8,128)(2,1)S(1)}, u32[]{:S(2)}, u32[]{:S(2)}) collective-permute-start(bf16[32,1024]{1,0:T(8,128)(2,1)S(1)} %get-tuple-element.36), channel_id=1, source_target_pairs={{0,16},{4,20},{8,24},{12,28},{16,0},{20,4},{24,8},{28,12},{1,17},{... | collective-permute-start | bytes 196616 | tf_op jit(solution)/shard_map/ppermute | solution.py:27
  7.7 7.1 %collective-permute-start.2 = (bf16[32,1024]{1,0:T(8,128)(2,1)S(1)}, bf16[32,1024]{1,0:T(8,128)(2,1)S(1)}, u32[]{:S(2)}, u32[]{:S(2)}) collective-permute-start(bf16[32,1024]{1,0:T(8,128)(2,1)S(1)} %get-tuple-element.38), channel_id=1, source_target_pairs={{0,4},{4,0},{8,12},{12,8},{16,20},{20,16},{24,28},{28,24},{1,5},{5... | collective-permute-start | bytes 196616 | tf_op jit(solution)/shard_map/ppermute | solution.py:27
  9.2 7.7 %collective-permute-start.3 = (bf16[32,1024]{1,0:T(8,128)(2,1)S(1)}, bf16[32,1024]{1,0:T(8,128)(2,1)S(1)}, u32[]{:S(2)}, u32[]{:S(2)}) collective-permute-start(bf16[32,1024]{1,0:T(8,128)(2,1)S(1)} %get-tuple-element.40), channel_id=1, source_target_pairs={{0,12},{4,8},{8,4},{12,0},{16,28},{20,24},{24,20},{28,16},{1,13},{... | collective-permute-start | bytes 196616 | tf_op jit(solution)/shard_map/ppermute | solution.py:27
  10.8 8.6 %collective-permute-start.1 = (bf16[32,1024]{1,0:T(8,128)(2,1)S(1)}, bf16[32,1024]{1,0:T(8,128)(2,1)S(1)}, u32[]{:S(2)}, u32[]{:S(2)}) collective-permute-start(bf16[32,1024]{1,0:T(8,128)(2,1)S(1)} %get-tuple-element.37), channel_id=1, source_target_pairs={{0,20},{4,16},{8,28},{12,24},{16,4},{20,0},{24,12},{28,8},{1,21},{... | collective-permute-start | bytes 196616 | tf_op jit(solution)/shard_map/ppermute | solution.py:27
  12.0 8.0 %collective-permute-start.6 = (bf16[32,1024]{1,0:T(8,128)(2,1)S(1)}, bf16[32,1024]{1,0:T(8,128)(2,1)S(1)}, u32[]{:S(2)}, u32[]{:S(2)}) collective-permute-start(bf16[32,1024]{1,0:T(8,128)(2,1)S(1)} %after.5), channel_id=1, source_target_pairs={{0,24},{4,28},{8,16},{12,20},{16,8},{20,12},{24,0},{28,4},{1,25},{... | collective-permute-start | bytes 196616 | tf_op jit(solution)/shard_map/ppermute | solution.py:27
  14.9 7.1 %collective-permute-start.5 = (bf16[32,1024]{1,0:T(8,128)(2,1)S(1)}, bf16[32,1024]{1,0:T(8,128)(2,1)S(1)}, u32[]{:S(2)}, u32[]{:S(2)}) collective-permute-start(bf16[32,1024]{1,0:T(8,128)(2,1)S(1)} %after.4), channel_id=1, source_target_pairs={{0,28},{4,24},{8,20},{12,16},{16,12},{20,8},{24,4},{28,0},{1,29},{... | collective-permute-start | bytes 196616 | tf_op jit(solution)/shard_map/ppermute | solution.py:27
  16.9 5.0 %collective-permute-start.4 = (bf16[32,1024]{1,0:T(8,128)(2,1)S(1)}, bf16[32,1024]{1,0:T(8,128)(2,1)S(1)}, u32[]{:S(2)}, u32[]{:S(2)}) collective-permute-start(bf16[32,1024]{1,0:T(8,128)(2,1)S(1)} %after.3), channel_id=1, source_target_pairs={{0,8},{4,12},{8,0},{12,4},{16,24},{20,28},{24,16},{28,20},{1,9},{5... | collective-permute-start | bytes 196616 | tf_op jit(solution)/shard_map/ppermute | solution.py:27
  19.5 7.9 %collective-permute-start.8 = (bf16[128,1024]{1,0:T(8,128)(2,1)S(1)}, bf16[128,1024]{1,0:T(8,128)(2,1)S(1)}, u32[]{:S(2)}, u32[]{:S(2)}) collective-permute-start(bf16[128,1024]{1,0:T(8,128)(2,1)S(1)} %half.2.refs_4_.first_ref), channel_id=1, source_target_pairs={{0,2},{1,3},{2,0},{3,1},{4,6},{5,7},{6,4},{7,5},{8,10},{9,11},{10,... | collective-permute-start | bytes 786440 | tf_op jit(solution)/shard_map/ppermute | solution.py:27
  22.0 8.2 %collective-permute-start.9 = (bf16[128,1024]{1,0:T(8,128)(2,1)S(1)}, bf16[128,1024]{1,0:T(8,128)(2,1)S(1)}, u32[]{:S(2)}, u32[]{:S(2)}) collective-permute-start(bf16[128,1024]{1,0:T(8,128)(2,1)S(1)} %half.3.refs_5_.second_ref), channel_id=1, source_target_pairs={{0,2},{1,3},{2,0},{3,1},{4,6},{5,7},{6,4},{7,5},{8,10},{9,11},{10,... | collective-permute-start | bytes 786440 | tf_op jit(solution)/shard_map/ppermute | solution.py:27
  25.4 6.3 %collective-permute-start.12 = (bf16[256,1024]{1,0:T(8,128)(2,1)S(1)}, bf16[256,1024]{1,0:T(8,128)(2,1)S(1)}, u32[]{:S(2)}, u32[]{:S(2)}) collective-permute-start(bf16[256,1024]{1,0:T(8,128)(2,1)S(1)} %get-tuple-element.48.refs_4_), channel_id=1, source_target_pairs={{0,1},{1,0},{2,3},{3,2},{4,5},{5,4},{6,7},{7,6},{8,9},{9,8},{10,11... | collective-permute-start | bytes 1572872 | tf_op jit(solution)/shard_map/ppermute | solution.py:27
  25.5 6.3 %collective-permute-start.7 = (bf16[256,1024]{1,0:T(8,128)(2,1)S(1)}, bf16[256,1024]{1,0:T(8,128)(2,1)S(1)}, u32[]{:S(2)}, u32[]{:S(2)}) collective-permute-start(bf16[256,1024]{1,0:T(8,128)(2,1)S(1)} %join.3.refs_0_), channel_id=1, source_target_pairs={{0,1},{1,0},{2,3},{3,2},{4,5},{5,4},{6,7},{7,6},{8,9},{9,8},{10,11... | collective-permute-start | bytes 1572872 | tf_op jit(solution)/shard_map/ppermute | solution.py:27
  26.0 5.8 %collective-permute-start.14 = (bf16[256,1024]{1,0:T(8,128)(2,1)S(1)}, bf16[256,1024]{1,0:T(8,128)(2,1)S(1)}, u32[]{:S(2)}, u32[]{:S(2)}) collective-permute-start(bf16[256,1024]{1,0:T(8,128)(2,1)S(1)} %collective-permute-done.13.refs_6_), channel_id=1, source_target_pairs={{0,1},{1,0},{2,3},{3,2},{4,5},{5,4},{6,7},{7,6},{8,9},{9,8},{10,11... | collective-permute-start | bytes 1572872 | tf_op jit(solution)/shard_map/ppermute | solution.py:27
  27.4 2.9 %collective-permute-start.10 = (bf16[128,1024]{1,0:T(8,128)(2,1)S(1)}, bf16[128,1024]{1,0:T(8,128)(2,1)S(1)}, u32[]{:S(2)}, u32[]{:S(2)}) collective-permute-start(bf16[128,1024]{1,0:T(8,128)(2,1)S(1)} %collective-permute-done.8.first_ref), channel_id=1, source_target_pairs={{0,1},{1,0},{2,3},{3,2},{4,5},{5,4},{6,7},{7,6},{8,9},{9,8},{10,11... | collective-permute-start | bytes 786440 | tf_op jit(solution)/shard_map/ppermute | solution.py:27
  33.5 3.6 %collective-permute-start.17 = (f32[8,128]{1,0:T(8,128)S(1)}, f32[8,128]{1,0:T(8,128)S(1)}, u32[]{:S(2)}, u32[]{:S(2)}) collective-permute-start(f32[8,128]{1,0:T(8,128)S(1)} %get-tuple-element.50.refs_0_), channel_id=1, source_target_pairs={{0,3},{1,2},{2,1},{3,0},{4,7},{5,6},{6,5},{7,4},{8,11},{9,10},{10,... | collective-permute-start | bytes 12296 | tf_op jit(solution)/shard_map/ppermute | solution.py:27
  33.9 3.6 %collective-permute-start.16 = (f32[8,128]{1,0:T(8,128)S(1)}, f32[8,128]{1,0:T(8,128)S(1)}, u32[]{:S(2)}, u32[]{:S(2)}) collective-permute-start(f32[8,128]{1,0:T(8,128)S(1)} %get-tuple-element.50.refs_0_), channel_id=1, source_target_pairs={{0,2},{1,3},{2,0},{3,1},{4,6},{5,7},{6,4},{7,5},{8,10},{9,11},{10,... | collective-permute-start | bytes 12296 | tf_op jit(solution)/shard_map/ppermute | solution.py:27
  35.4 2.1 %collective-permute-start.15 = (f32[8,128]{1,0:T(8,128)S(1)}, f32[8,128]{1,0:T(8,128)S(1)}, u32[]{:S(2)}, u32[]{:S(2)}) collective-permute-start(f32[8,128]{1,0:T(8,128)S(1)} %get-tuple-element.50.refs_0_), channel_id=1, source_target_pairs={{0,1},{1,0},{2,3},{3,2},{4,5},{5,4},{6,7},{7,6},{8,9},{9,8},{10,11... | collective-permute-start | bytes 12296 | tf_op jit(solution)/shard_map/ppermute | solution.py:27
  37.6 9.2 %collective-permute-start.21 = (bf16[32,1024]{1,0:T(8,128)(2,1)S(1)}, bf16[32,1024]{1,0:T(8,128)(2,1)S(1)}, u32[]{:S(2)}, u32[]{:S(2)}) collective-permute-start(bf16[32,1024]{1,0:T(8,128)(2,1)S(1)} %get-tuple-element.55), channel_id=1, source_target_pairs={{0,16},{4,20},{8,24},{12,28},{16,0},{20,4},{24,8},{28,12},{1,17},{... | collective-permute-start | bytes 196616 | tf_op jit(solution)/shard_map/ppermute | solution.py:27
  39.3 7.5 %collective-permute-start.22 = (bf16[32,1024]{1,0:T(8,128)(2,1)S(1)}, bf16[32,1024]{1,0:T(8,128)(2,1)S(1)}, u32[]{:S(2)}, u32[]{:S(2)}) collective-permute-start(bf16[32,1024]{1,0:T(8,128)(2,1)S(1)} %get-tuple-element.56), channel_id=1, source_target_pairs={{0,4},{4,0},{8,12},{12,8},{16,20},{20,16},{24,28},{28,24},{1,5},{5... | collective-permute-start | bytes 196616 | tf_op jit(solution)/shard_map/ppermute | solution.py:27
  40.3 10.2 %collective-permute-start.23 = (bf16[32,1024]{1,0:T(8,128)(2,1)S(1)}, bf16[32,1024]{1,0:T(8,128)(2,1)S(1)}, u32[]{:S(2)}, u32[]{:S(2)}) collective-permute-start(bf16[32,1024]{1,0:T(8,128)(2,1)S(1)} %get-tuple-element.57), channel_id=1, source_target_pairs={{0,20},{4,16},{8,28},{12,24},{16,4},{20,0},{24,12},{28,8},{1,21},{... | collective-permute-start | bytes 196616 | tf_op jit(solution)/shard_map/ppermute | solution.py:27
  42.1 8.4 %collective-permute-start.24 = (bf16[32,1024]{1,0:T(8,128)(2,1)S(1)}, bf16[32,1024]{1,0:T(8,128)(2,1)S(1)}, u32[]{:S(2)}, u32[]{:S(2)}) collective-permute-start(bf16[32,1024]{1,0:T(8,128)(2,1)S(1)} %get-tuple-element.58), channel_id=1, source_target_pairs={{0,24},{4,28},{8,16},{12,20},{16,8},{20,12},{24,0},{28,4},{1,25},{... | collective-permute-start | bytes 196616 | tf_op jit(solution)/shard_map/ppermute | solution.py:27
  44.3 7.7 %collective-permute-start.18 = (bf16[32,1024]{1,0:T(8,128)(2,1)S(1)}, bf16[32,1024]{1,0:T(8,128)(2,1)S(1)}, u32[]{:S(2)}, u32[]{:S(2)}) collective-permute-start(bf16[32,1024]{1,0:T(8,128)(2,1)S(1)} %get-tuple-element.52), channel_id=1, source_target_pairs={{0,28},{4,24},{8,20},{12,16},{16,12},{20,8},{24,4},{28,0},{1,29},{... | collective-permute-start | bytes 196616 | tf_op jit(solution)/shard_map/ppermute | solution.py:27
  46.8 5.9 %collective-permute-start.19 = (bf16[32,1024]{1,0:T(8,128)(2,1)S(1)}, bf16[32,1024]{1,0:T(8,128)(2,1)S(1)}, u32[]{:S(2)}, u32[]{:S(2)}) collective-permute-start(bf16[32,1024]{1,0:T(8,128)(2,1)S(1)} %get-tuple-element.53), channel_id=1, source_target_pairs={{0,12},{4,8},{8,4},{12,0},{16,28},{20,24},{24,20},{28,16},{1,13},{... | collective-permute-start | bytes 196616 | tf_op jit(solution)/shard_map/ppermute | solution.py:27
  46.8 5.9 %collective-permute-start.20 = (bf16[32,1024]{1,0:T(8,128)(2,1)S(1)}, bf16[32,1024]{1,0:T(8,128)(2,1)S(1)}, u32[]{:S(2)}, u32[]{:S(2)}) collective-permute-start(bf16[32,1024]{1,0:T(8,128)(2,1)S(1)} %get-tuple-element.54), channel_id=1, source_target_pairs={{0,8},{4,12},{8,0},{12,4},{16,24},{20,28},{24,16},{28,20},{1,9},{5... | collective-permute-start | bytes 196616 | tf_op jit(solution)/shard_map/ppermute | solution.py:27
  (1 other events, 1.5 us)

commit v3 on v2

--- a/solution.py
+++ b/solution.py
@@ -205,9 +205,8 @@
     )(product, *sums, *map(in_hbm, early))
 
 
-def stats_kernel(members, rows_side, old_ref, *refs):
-    g_refs = refs[:members]
-    new_out, new_mem, sems = refs[members:]
+def start_statistic(rows_side, old_ref, g_refs, new_out, new_mem, sems):
+    members = len(g_refs)
     member = lax.axis_index("rep")
     q, width = old_ref.shape
     step = 0.05 / width
@@ -230,7 +229,11 @@
         new_mem[j] = 0.95 * old_ref[:, cols] + step * product
         stores.append(pltpu.make_async_copy(new_mem.at[j], new_out.at[:, cols], sems.at[j]))
         stores[-1].start()
-    for store in stores:
+    return stores
+
+
+def stats_kernel(members, rows_side, old_ref, *refs):
+    for store in start_statistic(rows_side, old_ref, refs[:members], *refs[members:]):
         store.wait()
 
 
@@ -304,13 +307,18 @@
     )(*[in_hbm(a) for a in (owner, z, x, *wholes)], *early)
 
 
-def update_kernel(distances, fresh, block_ref, z_ref, x_ref, *refs):
+def update_kernel(distances, members, block_ref, z_ref, x_ref, *refs):
     n = len(distances)
-    back, outs = refs[:n], refs[n : n + 3] if fresh else refs[n + 3 : n + 6]
-    z_mem, x_mem, y_mem, sems = refs[-4:]
+    back, refs = refs[:n], refs[n:]
+    stores = []
+    if members:
+        outs, (z_mem, x_mem, y_mem, sems) = refs[members + 1 : members + 4], refs[-6:-2]
+        new_out = refs[members + 4]
+        stores += start_statistic(False, refs[0], refs[1 : members + 1], new_out, *refs[-2:])
+    else:
+        outs, (z_mem, x_mem, y_mem, sems) = refs[3:6], refs[-4:]
     width = z_ref.shape[2]
     blocks = [block_ref[d, 0] for d in distances]
-    stores = []
     for k, d in enumerate(distances):
         z_new = z_ref[d] - 0.2 * back[k][...].astype(F32)
         x_new = 0.75 * x_ref[d] + 0.25 * z_new
@@ -326,31 +334,37 @@
         store.wait()
 
 
-def update(block, z, x, back, distances, held=None):
+def update(block, z, x, back, distances, held=None, stat=()):
     count, rows, width = z.shape
     flat = (rows, count * width)
     n = len(distances)
     fresh = held is None
-    return pl.pallas_call(
-        functools.partial(update_kernel, distances, fresh),
+    extra = []
+    if stat:
+        members, q = len(stat) - 1, stat[0].shape[0]
+        extra = [pltpu.VMEM((members, q, q), F32), pltpu.SemaphoreType.DMA((members,))]
+    return pl.pallas_call(
+        functools.partial(update_kernel, distances, len(stat[1:])),
         out_shape=[
             jax.ShapeDtypeStruct(flat, F32),
             jax.ShapeDtypeStruct(flat, F32),
             jax.ShapeDtypeStruct(flat, BF16),
-        ],
-        in_specs=[VMEM] * (3 + n) + ([] if fresh else [HBM] * 3),
-        out_specs=[HBM] * 3,
+        ]
+        + [jax.ShapeDtypeStruct(old.shape, F32) for old in stat[:1]],
+        in_specs=[VMEM] * (3 + n) + [VMEM] * len(stat) + ([] if fresh else [HBM] * 3),
+        out_specs=[HBM] * (4 if stat else 3),
         input_output_aliases={} if fresh else {3 + n + i: i for i in range(3)},
         scratch_shapes=[
             pltpu.VMEM((n, rows, width), F32),
             pltpu.VMEM((n, rows, width), F32),
             pltpu.VMEM((n, rows, width), BF16),
             pltpu.SemaphoreType.DMA((3, n)),
-        ],
+        ]
+        + extra,
         compiler_params=params(16),
         cost_estimate=cost(8 * n * rows * width, 20 * n * rows * width),
         name="update",
-    )(block, z, x, *[back[d] for d in distances], *([] if fresh else held))
+    )(block, z, x, *[back[d] for d in distances], *stat, *([] if fresh else held))
 
 
 def gather_members(own, members):
@@ -402,10 +416,9 @@
     back = {0: piece[0]}
     for d in (4, 1, 5, 6, 7, 3, 2):
         back[d] = send(piece[d], d)
-    new = None
-    for distances in ((4, 1, 5, 6, 0), (7, 3, 2)):
-        new = update(block, z, x, back, distances, new)
-    return (*new, left_new, statistic(stat_right, blocks, False))
+    *new, right_new = update(block, z, x, back, (4, 1, 5, 6, 0), None, (stat_right, *blocks))
+    new = update(block, z, x, back, (7, 3, 2), new)
+    return (*new, left_new, right_new)
 
 
 def any_shape(flat, z, x, owner, stat_left, stat_right, root_left, root_right, count, members):

time: 53.9 us -> 53.9 us (level)
  Pallas kernels: 11.9 us -> 11.2 us
  waiting for transfers between devices: 11.2 us -> 11.9 us
    pallas_call x2 -> x1, Pallas kernels: 3.3 us -> 1.66 us  [statistic(): pl.pallas_call(functools.partial(stats_kernel, members, rows_side), out_s...]
    pallas_call x2, Pallas kernels: 2.36 us -> 3.33 us  [update(): pl.pallas_call(functools.partial(update_kernel, distances, len(stat[1:]))...]
    ppermute x25, waiting for transfers between devices: 11.2 us -> 11.9 us  [swap(): return lax.ppermute(x, axis, [(i, i ^ bit) for i in range(size)])]
  transfers between devices with their start and end apart: 25 -> 25, of which waited for: 8 -> 8; matrix products, arithmetic and copies ran while one was open for 0% -> 0% of each run, Pallas kernels for 17% -> 16%
where the time goes in v3:
time: 53.9 us; the launch traced here: 53.7 us
  starting transfers between devices  29.8 us (55%)
  waiting for transfers between devices  11.9 us (22%)
  Pallas kernels  11.2 us (21%)
  between operations  0.8 us (1%)
    ppermute x25, starting transfers between devices, swap(): return lax.ppermute(x, axis, [(i, i ^ bit) for i in range(size)])  29.8 us
    ppermute x25, waiting for transfers between devices, swap(): return lax.ppermute(x, axis, [(i, i ^ bit) for i in range(size)])  11.9 us
    pallas_call x2, Pallas kernels, update(): pl.pallas_call(functools.partial(update_kernel, distances, len(stat[1:]))...  3.33 us
    pallas_call x1, Pallas kernels, stage(): pl.pallas_call(functools.partial(stage_kernel, n), out_shape=[jax.ShapeDt...  2.82 us
    pallas_call x1, Pallas kernels, precondition(): pl.pallas_call(functools.partial(precond_kernel, members), out_shape=[jax...  1.73 us
    pallas_call x1, Pallas kernels, statistic(): pl.pallas_call(functools.partial(stats_kernel, members, rows_side), out_s...  1.66 us
    pallas_call x1, Pallas kernels, route(): pl.pallas_call(route_kernel, out_shape=[jax.ShapeDtypeStruct((rows, width...  1.37 us
  transfers between devices with their start and end apart: 25, of which 8 were waited for; matrix products, arithmetic and copies ran while one was open for 0% of the time, Pallas kernels for 16%

profile of v3, /device:TPU:0, one launch (start us, length us, event | category | flops | bytes accessed | tf_op | source)
XLA Modules:
  0.0 53.7 jit_solution(15151114175989737890)
XLA Ops:
  0.6 3.0 %collective-permute-start.13 = (bf16[256,1024]{1,0:T(8,128)(2,1)}, bf16[256,1024]{1,0:T(8,128)(2,1)S(1)}, u32[]{:S(2)}, u32[]{:S(2)}) collective-permute-start(bf16[256,1024]{1,0:T(8,128)(2,1)} %bitcast.21), channel_id=1, source_target_pairs={{0,2},{1,3},{2,0},{3,1},{4,6},{5,7},{6,4},{7,5},{8,10},{9,11},{10,... | collective-permute-start | bytes 1572872 | tf_op jit(solution)/shard_map/ppermute | solution.py:27
  3.7 1.4 %route.1 = (bf16[32,1024]{1,0:T(8,128)(2,1)S(1)}, bf16[32,1024]{1,0:T(8,128)(2,1)S(1)}, bf16[32,1024]{1,0:T(8,128)(2,1)S(1)}, bf16[32,1024]{1,0:T(8,128)(2,1)S(1...) custom-call(s32[8]{0:T(128)} %owner_ref.3, ...), custom_call_target="tpu_custom_call" | custom-call | bytes 1572864 | tf_op jit(solution)/shard_map/route/pallas_call | solution.py:64
  5.0 2.7 %collective-permute-start = (bf16[32,1024]{1,0:T(8,128)(2,1)S(1)}, bf16[32,1024]{1,0:T(8,128)(2,1)S(1)}, u32[]{:S(2)}, u32[]{:S(2)}) collective-permute-start(bf16[32,1024]{1,0:T(8,128)(2,1)S(1)} %get-tuple-element.37), channel_id=1, source_target_pairs={{0,16},{4,20},{8,24},{12,28},{16,0},{20,4},{24,8},{28,12},{1,17},{... | collective-permute-start | bytes 196616 | tf_op jit(solution)/shard_map/ppermute | solution.py:27
  7.7 1.5 %collective-permute-start.2 = (bf16[32,1024]{1,0:T(8,128)(2,1)S(1)}, bf16[32,1024]{1,0:T(8,128)(2,1)S(1)}, u32[]{:S(2)}, u32[]{:S(2)}) collective-permute-start(bf16[32,1024]{1,0:T(8,128)(2,1)S(1)} %get-tuple-element.39), channel_id=1, source_target_pairs={{0,4},{4,0},{8,12},{12,8},{16,20},{20,16},{24,28},{28,24},{1,5},{5... | collective-permute-start | bytes 196616 | tf_op jit(solution)/shard_map/ppermute | solution.py:27
  9.2 1.6 %collective-permute-start.3 = (bf16[32,1024]{1,0:T(8,128)(2,1)S(1)}, bf16[32,1024]{1,0:T(8,128)(2,1)S(1)}, u32[]{:S(2)}, u32[]{:S(2)}) collective-permute-start(bf16[32,1024]{1,0:T(8,128)(2,1)S(1)} %get-tuple-element.41), channel_id=1, source_target_pairs={{0,12},{4,8},{8,4},{12,0},{16,28},{20,24},{24,20},{28,16},{1,13},{... | collective-permute-start | bytes 196616 | tf_op jit(solution)/shard_map/ppermute | solution.py:27
  10.8 1.2 %collective-permute-start.1 = (bf16[32,1024]{1,0:T(8,128)(2,1)S(1)}, bf16[32,1024]{1,0:T(8,128)(2,1)S(1)}, u32[]{:S(2)}, u32[]{:S(2)}) collective-permute-start(bf16[32,1024]{1,0:T(8,128)(2,1)S(1)} %get-tuple-element.38), channel_id=1, source_target_pairs={{0,20},{4,16},{8,28},{12,24},{16,4},{20,0},{24,12},{28,8},{1,21},{... | collective-permute-start | bytes 196616 | tf_op jit(solution)/shard_map/ppermute | solution.py:27
  12.0 2.8 %collective-permute-start.6 = (bf16[32,1024]{1,0:T(8,128)(2,1)S(1)}, bf16[32,1024]{1,0:T(8,128)(2,1)S(1)}, u32[]{:S(2)}, u32[]{:S(2)}) collective-permute-start(bf16[32,1024]{1,0:T(8,128)(2,1)S(1)} %after.5), channel_id=1, source_target_pairs={{0,24},{4,28},{8,16},{12,20},{16,8},{20,12},{24,0},{28,4},{1,25},{... | collective-permute-start | bytes 196616 | tf_op jit(solution)/shard_map/ppermute | solution.py:27
  14.8 2.1 %collective-permute-start.5 = (bf16[32,1024]{1,0:T(8,128)(2,1)S(1)}, bf16[32,1024]{1,0:T(8,128)(2,1)S(1)}, u32[]{:S(2)}, u32[]{:S(2)}) collective-permute-start(bf16[32,1024]{1,0:T(8,128)(2,1)S(1)} %after.4), channel_id=1, source_target_pairs={{0,28},{4,24},{8,20},{12,16},{16,12},{20,8},{24,4},{28,0},{1,29},{... | collective-permute-start | bytes 196616 | tf_op jit(solution)/shard_map/ppermute | solution.py:27
  16.9 2.6 %collective-permute-done.1.refs_1_ = bf16[32,1024]{1,0:T(8,128)(2,1)S(1)} collective-permute-done((bf16[32,1024]{1,0:T(8,128)(2,1)S(1)}, bf16[32,1024]{1,0:T(8,128)(2,1)S(1)}, u32[]{:S(2)}, u32[]{:S(2)}) %collective-permute-start.1) | collective-permute-done | bytes 65568 | tf_op jit(solution)/shard_map/ppermute | solution.py:27
  20.1 1.8 %collective-permute-done.5.refs_2_ = bf16[32,1024]{1,0:T(8,128)(2,1)S(1)} collective-permute-done((bf16[32,1024]{1,0:T(8,128)(2,1)S(1)}, bf16[32,1024]{1,0:T(8,128)(2,1)S(1)}, u32[]{:S(2)}, u32[]{:S(2)}) %collective-permute-start.5) | collective-permute-done | bytes 65568 | tf_op jit(solution)/shard_map/ppermute | solution.py:27
  22.5 2.8 %stage.1 = (bf16[256,1024]{1,0:T(8,128)(2,1)S(1)}, bf16[256,1024]{1,0:T(8,128)(2,1)S(1)}, f32[256,1024]{1,0:T(8,128)S(1)}, f32[256,1024]{1,0:T(8,128)S(1)}, f32[...) custom-call(s32[8]{0:T(128)} %owner_ref.3, f32[32,8192]{1,0:T(8,128)} %bitcast.14, ...), custom_call_target="tpu_custom_call" | custom-call | bytes 10485760 | tf_op jit(solution)/shard_map/stage/pallas_call | solution.py:289
  26.1 1.4 %collective-permute-done.8.first_ref = bf16[128,1024]{1,0:T(8,128)(2,1)S(1)} collective-permute-done((bf16[128,1024]{1,0:T(8,128)(2,1)S(1)}, bf16[128,1024]{1,0:T(8,128)(2,1)S(1)}, u32[]{:S(2)}, u32[]{:S(2)}) %collective-permute-start.8) | collective-permute-done | bytes 262176 | tf_op jit(solution)/shard_map/ppermute | solution.py:27
  27.5 2.8 %collective-permute-done.9.second_ref = bf16[128,1024]{1,0:T(8,128)(2,1)S(1)} collective-permute-done((bf16[128,1024]{1,0:T(8,128)(2,1)S(1)}, bf16[128,1024]{1,0:T(8,128)(2,1)S(1)}, u32[]{:S(2)}, u32[]{:S(2)}) %collective-permute-start.9) | collective-permute-done | bytes 262176 | tf_op jit(solution)/shard_map/ppermute | solution.py:27
  30.3 1.5 %collective-permute-done.11.second_ref = bf16[128,1024]{1,0:T(8,128)(2,1)S(1)} collective-permute-done((bf16[128,1024]{1,0:T(8,128)(2,1)S(1)}, bf16[128,1024]{1,0:T(8,128)(2,1)S(1)}, u32[]{:S(2)}, u32[]{:S(2)}) %collective-permute-start.11) | collective-permute-done | bytes 262176 | tf_op jit(solution)/shard_map/ppermute | solution.py:27
  31.9 1.7 %precondition.1 = (f32[256,1024]{1,0:T(8,128)S(1)}, f32[8,128]{1,0:T(8,128)S(1)}) custom-call(bf16[256,1024]{1,0:T(8,128)(2,1)S(1)} %get-tuple-element.48.left_ref, bf16[256,1024]{1,0:T(8,128)(2,1)S(1)} %join.3.refs_0_.refs_6_, bf16[256,1024]{1,0:T(8,128)(2,1)S(1)} %collective-permute-done.7.refs_1_.refs_7_, bf16[256,1024]{1,0:T(8,128)(2,1)S(1)} %join.4.refs_2_.refs_8_, ...), custom_call_target="tpu_custom_call" | custom-call | flops 1073741824 | bytes 5242880 | tf_op jit(solution)/shard_map/precondition/pallas_call | solution.py:169
  33.9 1.5 %collective-permute-start.16 = (f32[8,128]{1,0:T(8,128)S(1)}, f32[8,128]{1,0:T(8,128)S(1)}, u32[]{:S(2)}, u32[]{:S(2)}) collective-permute-start(f32[8,128]{1,0:T(8,128)S(1)} %get-tuple-element.51.refs_0_), channel_id=1, source_target_pairs={{0,2},{1,3},{2,0},{3,1},{4,6},{5,7},{6,4},{7,5},{8,10},{9,11},{10,... | collective-permute-start | bytes 12296 | tf_op jit(solution)/shard_map/ppermute | solution.py:27
  35.5 1.7 %left_statistic.1.refs_4_ = f32[256,1024]{1,0:T(8,128)} custom-call(f32[256,1024]{1,0:T(8,128)S(1)} %get-tuple-element.52.old_ref, bf16[256,1024]{1,0:T(8,128)(2,1)S(1)} %join.3.refs_0_.refs_6_, bf16[256,1024]{1,0:T(8,128)(2,1)S(1)} %collective-permute-done.7.refs_1_.refs_7_, bf16[256,1024]{1,0:T(8,128)(2,1)S(1)} %join.4.refs_2_.refs_8_, ...), custom_call_target="tpu_custom_call" | custom-call | flops 536870912 | bytes 4194304 | tf_op jit(solution)/shard_map/left_statistic/pallas_call | solution.py:243
  37.7 1.6 %collective-permute-start.21 = (bf16[32,1024]{1,0:T(8,128)(2,1)S(1)}, bf16[32,1024]{1,0:T(8,128)(2,1)S(1)}, u32[]{:S(2)}, u32[]{:S(2)}) collective-permute-start(bf16[32,1024]{1,0:T(8,128)(2,1)S(1)} %get-tuple-element.56), channel_id=1, source_target_pairs={{0,16},{4,20},{8,24},{12,28},{16,0},{20,4},{24,8},{28,12},{1,17},{... | collective-permute-start | bytes 196616 | tf_op jit(solution)/shard_map/ppermute | solution.py:27
  40.3 1.8 %collective-permute-start.23 = (bf16[32,1024]{1,0:T(8,128)(2,1)S(1)}, bf16[32,1024]{1,0:T(8,128)(2,1)S(1)}, u32[]{:S(2)}, u32[]{:S(2)}) collective-permute-start(bf16[32,1024]{1,0:T(8,128)(2,1)S(1)} %get-tuple-element.58), channel_id=1, source_target_pairs={{0,20},{4,16},{8,28},{12,24},{16,4},{20,0},{24,12},{28,8},{1,21},{... | collective-permute-start | bytes 196616 | tf_op jit(solution)/shard_map/ppermute | solution.py:27
  42.1 2.2 %collective-permute-start.24 = (bf16[32,1024]{1,0:T(8,128)(2,1)S(1)}, bf16[32,1024]{1,0:T(8,128)(2,1)S(1)}, u32[]{:S(2)}, u32[]{:S(2)}) collective-permute-start(bf16[32,1024]{1,0:T(8,128)(2,1)S(1)} %get-tuple-element.59), channel_id=1, source_target_pairs={{0,24},{4,28},{8,16},{12,20},{16,8},{20,12},{24,0},{28,4},{1,25},{... | collective-permute-start | bytes 196616 | tf_op jit(solution)/shard_map/ppermute | solution.py:27
  44.3 2.5 %collective-permute-start.18 = (bf16[32,1024]{1,0:T(8,128)(2,1)S(1)}, bf16[32,1024]{1,0:T(8,128)(2,1)S(1)}, u32[]{:S(2)}, u32[]{:S(2)}) collective-permute-start(bf16[32,1024]{1,0:T(8,128)(2,1)S(1)} %get-tuple-element.53), channel_id=1, source_target_pairs={{0,28},{4,24},{8,20},{12,16},{16,12},{20,8},{24,4},{28,0},{1,29},{... | collective-permute-start | bytes 196616 | tf_op jit(solution)/shard_map/ppermute | solution.py:27
  46.8 2.1 %collective-permute-start.20 = (bf16[32,1024]{1,0:T(8,128)(2,1)S(1)}, bf16[32,1024]{1,0:T(8,128)(2,1)S(1)}, u32[]{:S(2)}, u32[]{:S(2)}) collective-permute-start(bf16[32,1024]{1,0:T(8,128)(2,1)S(1)} %get-tuple-element.55), channel_id=1, source_target_pairs={{0,8},{4,12},{8,0},{12,4},{16,24},{20,28},{24,16},{28,20},{1,9},{5... | collective-permute-start | bytes 196616 | tf_op jit(solution)/shard_map/ppermute | solution.py:27
  48.9 1.1 %collective-permute-done.23.refs_2_ = bf16[32,1024]{1,0:T(8,128)(2,1)S(1)} collective-permute-done((bf16[32,1024]{1,0:T(8,128)(2,1)S(1)}, bf16[32,1024]{1,0:T(8,128)(2,1)S(1)}, u32[]{:S(2)}, u32[]{:S(2)}) %collective-permute-start.23) | collective-permute-done | bytes 65568 | tf_op jit(solution)/shard_map/ppermute | solution.py:27
  50.0 2.3 %update.2 = (f32[32,8192]{1,0:T(8,128)}, f32[32,8192]{1,0:T(8,128)}, bf16[32,8192]{1,0:T(8,128)(2,1)}, f32[256,1024]{1,0:T(8,128)}) custom-call(s32[8,128]{1,0:T(8,128)S(1)} %get-tuple-element.45.block_ref, f32[8,32,1024]{2,1,0:T(8,128)S(1)} %get-tuple-element.46.refs_0_.z_ref, f32[8,32,1024]{2,1,0:T(8,128)S(1)} %get-tuple-element.47.x_ref, ...), custom_call_target="tpu_custom_call" | custom-call | flops 1310720 | bytes 3276800 | tf_op jit(solution)/shard_map/update/pallas_call | solution.py:346
  (41 shorter events, 5.3 us)
Async XLA Ops:
  0.6 25.4 %collective-permute-start.13 = (bf16[256,1024]{1,0:T(8,128)(2,1)}, bf16[256,1024]{1,0:T(8,128)(2,1)S(1)}, u32[]{:S(2)}, u32[]{:S(2)}) collective-permute-start(bf16[256,1024]{1,0:T(8,128)(2,1)} %bitcast.21), channel_id=1, source_target_pairs={{0,2},{1,3},{2,0},{3,1},{4,6},{5,7},{6,4},{7,5},{8,10},{9,11},{10,... | collective-permute-start | bytes 1572872 | tf_op jit(solution)/shard_map/ppermute | solution.py:27
  5.0 7.0 %collective-permute-start = (bf16[32,1024]{1,0:T(8,128)(2,1)S(1)}, bf16[32,1024]{1,0:T(8,128)(2,1)S(1)}, u32[]{:S(2)}, u32[]{:S(2)}) collective-permute-start(bf16[32,1024]{1,0:T(8,128)(2,1)S(1)} %get-tuple-element.37), channel_id=1, source_target_pairs={{0,16},{4,20},{8,24},{12,28},{16,0},{20,4},{24,8},{28,12},{1,17},{... | collective-permute-start | bytes 196616 | tf_op jit(solution)/shard_map/ppermute | solution.py:27
  7.7 7.1 %collective-permute-start.2 = (bf16[32,1024]{1,0:T(8,128)(2,1)S(1)}, bf16[32,1024]{1,0:T(8,128)(2,1)S(1)}, u32[]{:S(2)}, u32[]{:S(2)}) collective-permute-start(bf16[32,1024]{1,0:T(8,128)(2,1)S(1)} %get-tuple-element.39), channel_id=1, source_target_pairs={{0,4},{4,0},{8,12},{12,8},{16,20},{20,16},{24,28},{28,24},{1,5},{5... | collective-permute-start | bytes 196616 | tf_op jit(solution)/shard_map/ppermute | solution.py:27
  9.2 7.7 %collective-permute-start.3 = (bf16[32,1024]{1,0:T(8,128)(2,1)S(1)}, bf16[32,1024]{1,0:T(8,128)(2,1)S(1)}, u32[]{:S(2)}, u32[]{:S(2)}) collective-permute-start(bf16[32,1024]{1,0:T(8,128)(2,1)S(1)} %get-tuple-element.41), channel_id=1, source_target_pairs={{0,12},{4,8},{8,4},{12,0},{16,28},{20,24},{24,20},{28,16},{1,13},{... | collective-permute-start | bytes 196616 | tf_op jit(solution)/shard_map/ppermute | solution.py:27
  10.8 8.7 %collective-permute-start.1 = (bf16[32,1024]{1,0:T(8,128)(2,1)S(1)}, bf16[32,1024]{1,0:T(8,128)(2,1)S(1)}, u32[]{:S(2)}, u32[]{:S(2)}) collective-permute-start(bf16[32,1024]{1,0:T(8,128)(2,1)S(1)} %get-tuple-element.38), channel_id=1, source_target_pairs={{0,20},{4,16},{8,28},{12,24},{16,4},{20,0},{24,12},{28,8},{1,21},{... | collective-permute-start | bytes 196616 | tf_op jit(solution)/shard_map/ppermute | solution.py:27
  12.0 8.1 %collective-permute-start.6 = (bf16[32,1024]{1,0:T(8,128)(2,1)S(1)}, bf16[32,1024]{1,0:T(8,128)(2,1)S(1)}, u32[]{:S(2)}, u32[]{:S(2)}) collective-permute-start(bf16[32,1024]{1,0:T(8,128)(2,1)S(1)} %after.5), channel_id=1, source_target_pairs={{0,24},{4,28},{8,16},{12,20},{16,8},{20,12},{24,0},{28,4},{1,25},{... | collective-permute-start | bytes 196616 | tf_op jit(solution)/shard_map/ppermute | solution.py:27
  14.8 7.1 %collective-permute-start.5 = (bf16[32,1024]{1,0:T(8,128)(2,1)S(1)}, bf16[32,1024]{1,0:T(8,128)(2,1)S(1)}, u32[]{:S(2)}, u32[]{:S(2)}) collective-permute-start(bf16[32,1024]{1,0:T(8,128)(2,1)S(1)} %after.4), channel_id=1, source_target_pairs={{0,28},{4,24},{8,20},{12,16},{16,12},{20,8},{24,4},{28,0},{1,29},{... | collective-permute-start | bytes 196616 | tf_op jit(solution)/shard_map/ppermute | solution.py:27
  16.9 5.0 %collective-permute-start.4 = (bf16[32,1024]{1,0:T(8,128)(2,1)S(1)}, bf16[32,1024]{1,0:T(8,128)(2,1)S(1)}, u32[]{:S(2)}, u32[]{:S(2)}) collective-permute-start(bf16[32,1024]{1,0:T(8,128)(2,1)S(1)} %after.3), channel_id=1, source_target_pairs={{0,8},{4,12},{8,0},{12,4},{16,24},{20,28},{24,16},{28,20},{1,9},{5... | collective-permute-start | bytes 196616 | tf_op jit(solution)/shard_map/ppermute | solution.py:27
  19.5 7.9 %collective-permute-start.8 = (bf16[128,1024]{1,0:T(8,128)(2,1)S(1)}, bf16[128,1024]{1,0:T(8,128)(2,1)S(1)}, u32[]{:S(2)}, u32[]{:S(2)}) collective-permute-start(bf16[128,1024]{1,0:T(8,128)(2,1)S(1)} %half.2.refs_4_.first_ref), channel_id=1, source_target_pairs={{0,2},{1,3},{2,0},{3,1},{4,6},{5,7},{6,4},{7,5},{8,10},{9,11},{10,... | collective-permute-start | bytes 786440 | tf_op jit(solution)/shard_map/ppermute | solution.py:27
  22.0 8.3 %collective-permute-start.9 = (bf16[128,1024]{1,0:T(8,128)(2,1)S(1)}, bf16[128,1024]{1,0:T(8,128)(2,1)S(1)}, u32[]{:S(2)}, u32[]{:S(2)}) collective-permute-start(bf16[128,1024]{1,0:T(8,128)(2,1)S(1)} %half.3.refs_5_.second_ref), channel_id=1, source_target_pairs={{0,2},{1,3},{2,0},{3,1},{4,6},{5,7},{6,4},{7,5},{8,10},{9,11},{10,... | collective-permute-start | bytes 786440 | tf_op jit(solution)/shard_map/ppermute | solution.py:27
  25.4 6.4 %collective-permute-start.12 = (bf16[256,1024]{1,0:T(8,128)(2,1)S(1)}, bf16[256,1024]{1,0:T(8,128)(2,1)S(1)}, u32[]{:S(2)}, u32[]{:S(2)}) collective-permute-start(bf16[256,1024]{1,0:T(8,128)(2,1)S(1)} %get-tuple-element.49.refs_4_), channel_id=1, source_target_pairs={{0,1},{1,0},{2,3},{3,2},{4,5},{5,4},{6,7},{7,6},{8,9},{9,8},{10,11... | collective-permute-start | bytes 1572872 | tf_op jit(solution)/shard_map/ppermute | solution.py:27
  25.5 6.4 %collective-permute-start.7 = (bf16[256,1024]{1,0:T(8,128)(2,1)S(1)}, bf16[256,1024]{1,0:T(8,128)(2,1)S(1)}, u32[]{:S(2)}, u32[]{:S(2)}) collective-permute-start(bf16[256,1024]{1,0:T(8,128)(2,1)S(1)} %join.3.refs_0_.refs_6_), channel_id=1, source_target_pairs={{0,1},{1,0},{2,3},{3,2},{4,5},{5,4},{6,7},{7,6},{8,9},{9,8},{10,11... | collective-permute-start | bytes 1572872 | tf_op jit(solution)/shard_map/ppermute | solution.py:27
  26.0 5.9 %collective-permute-start.14 = (bf16[256,1024]{1,0:T(8,128)(2,1)S(1)}, bf16[256,1024]{1,0:T(8,128)(2,1)S(1)}, u32[]{:S(2)}, u32[]{:S(2)}) collective-permute-start(bf16[256,1024]{1,0:T(8,128)(2,1)S(1)} %collective-permute-done.13.refs_6_), channel_id=1, source_target_pairs={{0,1},{1,0},{2,3},{3,2},{4,5},{5,4},{6,7},{7,6},{8,9},{9,8},{10,11... | collective-permute-start | bytes 1572872 | tf_op jit(solution)/shard_map/ppermute | solution.py:27
  27.5 2.9 %collective-permute-start.10 = (bf16[128,1024]{1,0:T(8,128)(2,1)S(1)}, bf16[128,1024]{1,0:T(8,128)(2,1)S(1)}, u32[]{:S(2)}, u32[]{:S(2)}) collective-permute-start(bf16[128,1024]{1,0:T(8,128)(2,1)S(1)} %collective-permute-done.8.first_ref), channel_id=1, source_target_pairs={{0,1},{1,0},{2,3},{3,2},{4,5},{5,4},{6,7},{7,6},{8,9},{9,8},{10,11... | collective-permute-start | bytes 786440 | tf_op jit(solution)/shard_map/ppermute | solution.py:27
  33.6 3.6 %collective-permute-start.17 = (f32[8,128]{1,0:T(8,128)S(1)}, f32[8,128]{1,0:T(8,128)S(1)}, u32[]{:S(2)}, u32[]{:S(2)}) collective-permute-start(f32[8,128]{1,0:T(8,128)S(1)} %get-tuple-element.51.refs_0_), channel_id=1, source_target_pairs={{0,3},{1,2},{2,1},{3,0},{4,7},{5,6},{6,5},{7,4},{8,11},{9,10},{10,... | collective-permute-start | bytes 12296 | tf_op jit(solution)/shard_map/ppermute | solution.py:27
  33.9 3.6 %collective-permute-start.16 = (f32[8,128]{1,0:T(8,128)S(1)}, f32[8,128]{1,0:T(8,128)S(1)}, u32[]{:S(2)}, u32[]{:S(2)}) collective-permute-start(f32[8,128]{1,0:T(8,128)S(1)} %get-tuple-element.51.refs_0_), channel_id=1, source_target_pairs={{0,2},{1,3},{2,0},{3,1},{4,6},{5,7},{6,4},{7,5},{8,10},{9,11},{10,... | collective-permute-start | bytes 12296 | tf_op jit(solution)/shard_map/ppermute | solution.py:27
  35.5 2.1 %collective-permute-start.15 = (f32[8,128]{1,0:T(8,128)S(1)}, f32[8,128]{1,0:T(8,128)S(1)}, u32[]{:S(2)}, u32[]{:S(2)}) collective-permute-start(f32[8,128]{1,0:T(8,128)S(1)} %get-tuple-element.51.refs_0_), channel_id=1, source_target_pairs={{0,1},{1,0},{2,3},{3,2},{4,5},{5,4},{6,7},{7,6},{8,9},{9,8},{10,11... | collective-permute-start | bytes 12296 | tf_op jit(solution)/shard_map/ppermute | solution.py:27
  37.7 9.1 %collective-permute-start.21 = (bf16[32,1024]{1,0:T(8,128)(2,1)S(1)}, bf16[32,1024]{1,0:T(8,128)(2,1)S(1)}, u32[]{:S(2)}, u32[]{:S(2)}) collective-permute-start(bf16[32,1024]{1,0:T(8,128)(2,1)S(1)} %get-tuple-element.56), channel_id=1, source_target_pairs={{0,16},{4,20},{8,24},{12,28},{16,0},{20,4},{24,8},{28,12},{1,17},{... | collective-permute-start | bytes 196616 | tf_op jit(solution)/shard_map/ppermute | solution.py:27
  39.3 7.5 %collective-permute-start.22 = (bf16[32,1024]{1,0:T(8,128)(2,1)S(1)}, bf16[32,1024]{1,0:T(8,128)(2,1)S(1)}, u32[]{:S(2)}, u32[]{:S(2)}) collective-permute-start(bf16[32,1024]{1,0:T(8,128)(2,1)S(1)} %get-tuple-element.57), channel_id=1, source_target_pairs={{0,4},{4,0},{8,12},{12,8},{16,20},{20,16},{24,28},{28,24},{1,5},{5... | collective-permute-start | bytes 196616 | tf_op jit(solution)/shard_map/ppermute | solution.py:27
  40.3 9.7 %collective-permute-start.23 = (bf16[32,1024]{1,0:T(8,128)(2,1)S(1)}, bf16[32,1024]{1,0:T(8,128)(2,1)S(1)}, u32[]{:S(2)}, u32[]{:S(2)}) collective-permute-start(bf16[32,1024]{1,0:T(8,128)(2,1)S(1)} %get-tuple-element.58), channel_id=1, source_target_pairs={{0,20},{4,16},{8,28},{12,24},{16,4},{20,0},{24,12},{28,8},{1,21},{... | collective-permute-start | bytes 196616 | tf_op jit(solution)/shard_map/ppermute | solution.py:27
  42.1 7.8 %collective-permute-start.24 = (bf16[32,1024]{1,0:T(8,128)(2,1)S(1)}, bf16[32,1024]{1,0:T(8,128)(2,1)S(1)}, u32[]{:S(2)}, u32[]{:S(2)}) collective-permute-start(bf16[32,1024]{1,0:T(8,128)(2,1)S(1)} %get-tuple-element.59), channel_id=1, source_target_pairs={{0,24},{4,28},{8,16},{12,20},{16,8},{20,12},{24,0},{28,4},{1,25},{... | collective-permute-start | bytes 196616 | tf_op jit(solution)/shard_map/ppermute | solution.py:27
  44.3 7.9 %collective-permute-start.18 = (bf16[32,1024]{1,0:T(8,128)(2,1)S(1)}, bf16[32,1024]{1,0:T(8,128)(2,1)S(1)}, u32[]{:S(2)}, u32[]{:S(2)}) collective-permute-start(bf16[32,1024]{1,0:T(8,128)(2,1)S(1)} %get-tuple-element.53), channel_id=1, source_target_pairs={{0,28},{4,24},{8,20},{12,16},{16,12},{20,8},{24,4},{28,0},{1,29},{... | collective-permute-start | bytes 196616 | tf_op jit(solution)/shard_map/ppermute | solution.py:27
  46.8 5.9 %collective-permute-start.19 = (bf16[32,1024]{1,0:T(8,128)(2,1)S(1)}, bf16[32,1024]{1,0:T(8,128)(2,1)S(1)}, u32[]{:S(2)}, u32[]{:S(2)}) collective-permute-start(bf16[32,1024]{1,0:T(8,128)(2,1)S(1)} %get-tuple-element.54), channel_id=1, source_target_pairs={{0,12},{4,8},{8,4},{12,0},{16,28},{20,24},{24,20},{28,16},{1,13},{... | collective-permute-start | bytes 196616 | tf_op jit(solution)/shard_map/ppermute | solution.py:27
  46.8 5.9 %collective-permute-start.20 = (bf16[32,1024]{1,0:T(8,128)(2,1)S(1)}, bf16[32,1024]{1,0:T(8,128)(2,1)S(1)}, u32[]{:S(2)}, u32[]{:S(2)}) collective-permute-start(bf16[32,1024]{1,0:T(8,128)(2,1)S(1)} %get-tuple-element.55), channel_id=1, source_target_pairs={{0,8},{4,12},{8,0},{12,4},{16,24},{20,28},{24,16},{28,20},{1,9},{5... | collective-permute-start | bytes 196616 | tf_op jit(solution)/shard_map/ppermute | solution.py:27
  (1 other events, 1.5 us)

commit v4 on v3

--- a/solution.py
+++ b/solution.py
@@ -416,8 +416,9 @@
     back = {0: piece[0]}
     for d in (4, 1, 5, 6, 7, 3, 2):
         back[d] = send(piece[d], d)
-    *new, right_new = update(block, z, x, back, (4, 1, 5, 6, 0), None, (stat_right, *blocks))
-    new = update(block, z, x, back, (7, 3, 2), new)
+    *new, right_new = update(block, z, x, back, (4, 1, 5, 0), None, (stat_right, *blocks))
+    for distances in ((6, 3), (7, 2)):
+        new = update(block, z, x, back, distances, new)
     return (*new, left_new, right_new)
 
 

time: 53.9 us -> 53.5 us (level)
  starting transfers between devices: 29.8 us -> 28.6 us
  Pallas kernels: 11.2 us -> 11.9 us
    ppermute x25, starting transfers between devices: 29.8 us -> 28.6 us  [swap(): return lax.ppermute(x, axis, [(i, i ^ bit) for i in range(size)])]
    pallas_call x2 -> x3, Pallas kernels: 3.33 us -> 3.98 us  [update(): pl.pallas_call(functools.partial(update_kernel, distances, len(stat[1:]))...]
  transfers between devices with their start and end apart: 25 -> 25, of which waited for: 8 -> 8; matrix products, arithmetic and copies ran while one was open for 0% -> 0% of each run, Pallas kernels for 16% -> 17%
where the time goes in v4:
time: 53.5 us; the launch traced here: 53.4 us
  starting transfers between devices  28.6 us (53%)
  waiting for transfers between devices  12.1 us (23%)
  Pallas kernels  11.9 us (22%)
  between operations  0.83 us (2%)
    ppermute x25, starting transfers between devices, swap(): return lax.ppermute(x, axis, [(i, i ^ bit) for i in range(size)])  28.6 us
    ppermute x25, waiting for transfers between devices, swap(): return lax.ppermute(x, axis, [(i, i ^ bit) for i in range(size)])  12.1 us
    pallas_call x3, Pallas kernels, update(): pl.pallas_call(functools.partial(update_kernel, distances, len(stat[1:]))...  3.98 us
    pallas_call x1, Pallas kernels, stage(): pl.pallas_call(functools.partial(stage_kernel, n), out_shape=[jax.ShapeDt...  2.82 us
    pallas_call x1, Pallas kernels, precondition(): pl.pallas_call(functools.partial(precond_kernel, members), out_shape=[jax...  1.72 us
    pallas_call x1, Pallas kernels, statistic(): pl.pallas_call(functools.partial(stats_kernel, members, rows_side), out_s...  1.65 us
    pallas_call x1, Pallas kernels, route(): pl.pallas_call(route_kernel, out_shape=[jax.ShapeDtypeStruct((rows, width...  1.38 us
  transfers between devices with their start and end apart: 25, of which 8 were waited for; matrix products, arithmetic and copies ran while one was open for 0% of the time, Pallas kernels for 17%

profile of v4, /device:TPU:0, one launch (start us, length us, event | category | flops | bytes accessed | tf_op | source)
XLA Modules:
  0.0 53.4 jit_solution(202554752793357689)
XLA Ops:
  0.6 3.0 %collective-permute-start.13 = (bf16[256,1024]{1,0:T(8,128)(2,1)}, bf16[256,1024]{1,0:T(8,128)(2,1)S(1)}, u32[]{:S(2)}, u32[]{:S(2)}) collective-permute-start(bf16[256,1024]{1,0:T(8,128)(2,1)} %bitcast.22), channel_id=1, source_target_pairs={{0,2},{1,3},{2,0},{3,1},{4,6},{5,7},{6,4},{7,5},{8,10},{9,11},{10,... | collective-permute-start | bytes 1572872 | tf_op jit(solution)/shard_map/ppermute | solution.py:27
  3.7 1.4 %route.1 = (bf16[32,1024]{1,0:T(8,128)(2,1)S(1)}, bf16[32,1024]{1,0:T(8,128)(2,1)S(1)}, bf16[32,1024]{1,0:T(8,128)(2,1)S(1)}, bf16[32,1024]{1,0:T(8,128)(2,1)S(1...) custom-call(s32[8]{0:T(128)} %owner_ref.3, ...), custom_call_target="tpu_custom_call" | custom-call | bytes 1572864 | tf_op jit(solution)/shard_map/route/pallas_call | solution.py:64
  5.0 2.7 %collective-permute-start = (bf16[32,1024]{1,0:T(8,128)(2,1)S(1)}, bf16[32,1024]{1,0:T(8,128)(2,1)S(1)}, u32[]{:S(2)}, u32[]{:S(2)}) collective-permute-start(bf16[32,1024]{1,0:T(8,128)(2,1)S(1)} %get-tuple-element.40), channel_id=1, source_target_pairs={{0,16},{4,20},{8,24},{12,28},{16,0},{20,4},{24,8},{28,12},{1,17},{... | collective-permute-start | bytes 196616 | tf_op jit(solution)/shard_map/ppermute | solution.py:27
  7.7 1.5 %collective-permute-start.2 = (bf16[32,1024]{1,0:T(8,128)(2,1)S(1)}, bf16[32,1024]{1,0:T(8,128)(2,1)S(1)}, u32[]{:S(2)}, u32[]{:S(2)}) collective-permute-start(bf16[32,1024]{1,0:T(8,128)(2,1)S(1)} %get-tuple-element.42), channel_id=1, source_target_pairs={{0,4},{4,0},{8,12},{12,8},{16,20},{20,16},{24,28},{28,24},{1,5},{5... | collective-permute-start | bytes 196616 | tf_op jit(solution)/shard_map/ppermute | solution.py:27
  9.2 1.6 %collective-permute-start.3 = (bf16[32,1024]{1,0:T(8,128)(2,1)S(1)}, bf16[32,1024]{1,0:T(8,128)(2,1)S(1)}, u32[]{:S(2)}, u32[]{:S(2)}) collective-permute-start(bf16[32,1024]{1,0:T(8,128)(2,1)S(1)} %get-tuple-element.44), channel_id=1, source_target_pairs={{0,12},{4,8},{8,4},{12,0},{16,28},{20,24},{24,20},{28,16},{1,13},{... | collective-permute-start | bytes 196616 | tf_op jit(solution)/shard_map/ppermute | solution.py:27
  10.8 1.2 %collective-permute-start.1 = (bf16[32,1024]{1,0:T(8,128)(2,1)S(1)}, bf16[32,1024]{1,0:T(8,128)(2,1)S(1)}, u32[]{:S(2)}, u32[]{:S(2)}) collective-permute-start(bf16[32,1024]{1,0:T(8,128)(2,1)S(1)} %get-tuple-element.41), channel_id=1, source_target_pairs={{0,20},{4,16},{8,28},{12,24},{16,4},{20,0},{24,12},{28,8},{1,21},{... | collective-permute-start | bytes 196616 | tf_op jit(solution)/shard_map/ppermute | solution.py:27
  12.0 2.9 %collective-permute-start.6 = (bf16[32,1024]{1,0:T(8,128)(2,1)S(1)}, bf16[32,1024]{1,0:T(8,128)(2,1)S(1)}, u32[]{:S(2)}, u32[]{:S(2)}) collective-permute-start(bf16[32,1024]{1,0:T(8,128)(2,1)S(1)} %after.5), channel_id=1, source_target_pairs={{0,24},{4,28},{8,16},{12,20},{16,8},{20,12},{24,0},{28,4},{1,25},{... | collective-permute-start | bytes 196616 | tf_op jit(solution)/shard_map/ppermute | solution.py:27
  14.9 2.0 %collective-permute-start.5 = (bf16[32,1024]{1,0:T(8,128)(2,1)S(1)}, bf16[32,1024]{1,0:T(8,128)(2,1)S(1)}, u32[]{:S(2)}, u32[]{:S(2)}) collective-permute-start(bf16[32,1024]{1,0:T(8,128)(2,1)S(1)} %after.4), channel_id=1, source_target_pairs={{0,28},{4,24},{8,20},{12,16},{16,12},{20,8},{24,4},{28,0},{1,29},{... | collective-permute-start | bytes 196616 | tf_op jit(solution)/shard_map/ppermute | solution.py:27
  16.9 2.5 %collective-permute-done.1.refs_1_ = bf16[32,1024]{1,0:T(8,128)(2,1)S(1)} collective-permute-done((bf16[32,1024]{1,0:T(8,128)(2,1)S(1)}, bf16[32,1024]{1,0:T(8,128)(2,1)S(1)}, u32[]{:S(2)}, u32[]{:S(2)}) %collective-permute-start.1) | collective-permute-done | bytes 65568 | tf_op jit(solution)/shard_map/ppermute | solution.py:27
  20.0 1.9 %collective-permute-done.5.refs_2_ = bf16[32,1024]{1,0:T(8,128)(2,1)S(1)} collective-permute-done((bf16[32,1024]{1,0:T(8,128)(2,1)S(1)}, bf16[32,1024]{1,0:T(8,128)(2,1)S(1)}, u32[]{:S(2)}, u32[]{:S(2)}) %collective-permute-start.5) | collective-permute-done | bytes 65568 | tf_op jit(solution)/shard_map/ppermute | solution.py:27
  22.6 2.8 %stage.1 = (bf16[256,1024]{1,0:T(8,128)(2,1)S(1)}, bf16[256,1024]{1,0:T(8,128)(2,1)S(1)}, f32[256,1024]{1,0:T(8,128)S(1)}, f32[256,1024]{1,0:T(8,128)S(1)}, f32[...) custom-call(s32[8]{0:T(128)} %owner_ref.3, f32[32,8192]{1,0:T(8,128)} %bitcast.17, ...), custom_call_target="tpu_custom_call" | custom-call | bytes 10485760 | tf_op jit(solution)/shard_map/stage/pallas_call | solution.py:289
  26.1 1.3 %collective-permute-done.8.first_ref = bf16[128,1024]{1,0:T(8,128)(2,1)S(1)} collective-permute-done((bf16[128,1024]{1,0:T(8,128)(2,1)S(1)}, bf16[128,1024]{1,0:T(8,128)(2,1)S(1)}, u32[]{:S(2)}, u32[]{:S(2)}) %collective-permute-start.8) | collective-permute-done | bytes 262176 | tf_op jit(solution)/shard_map/ppermute | solution.py:27
  27.4 2.8 %collective-permute-done.9.second_ref = bf16[128,1024]{1,0:T(8,128)(2,1)S(1)} collective-permute-done((bf16[128,1024]{1,0:T(8,128)(2,1)S(1)}, bf16[128,1024]{1,0:T(8,128)(2,1)S(1)}, u32[]{:S(2)}, u32[]{:S(2)}) %collective-permute-start.9) | collective-permute-done | bytes 262176 | tf_op jit(solution)/shard_map/ppermute | solution.py:27
  30.3 1.5 %collective-permute-done.11.second_ref = bf16[128,1024]{1,0:T(8,128)(2,1)S(1)} collective-permute-done((bf16[128,1024]{1,0:T(8,128)(2,1)S(1)}, bf16[128,1024]{1,0:T(8,128)(2,1)S(1)}, u32[]{:S(2)}, u32[]{:S(2)}) %collective-permute-start.11) | collective-permute-done | bytes 262176 | tf_op jit(solution)/shard_map/ppermute | solution.py:27
  31.8 1.7 %precondition.1 = (f32[256,1024]{1,0:T(8,128)S(1)}, f32[8,128]{1,0:T(8,128)S(1)}) custom-call(bf16[256,1024]{1,0:T(8,128)(2,1)S(1)} %get-tuple-element.51.left_ref, bf16[256,1024]{1,0:T(8,128)(2,1)S(1)} %join.3.refs_0_.refs_5_, bf16[256,1024]{1,0:T(8,128)(2,1)S(1)} %collective-permute-done.7.refs_1_.refs_6_, bf16[256,1024]{1,0:T(8,128)(2,1)S(1)} %join.4.refs_2_.refs_7_, ...), custom_call_target="tpu_custom_call" | custom-call | flops 1073741824 | bytes 5242880 | tf_op jit(solution)/shard_map/precondition/pallas_call | solution.py:169
  33.9 1.5 %collective-permute-start.16 = (f32[8,128]{1,0:T(8,128)S(1)}, f32[8,128]{1,0:T(8,128)S(1)}, u32[]{:S(2)}, u32[]{:S(2)}) collective-permute-start(f32[8,128]{1,0:T(8,128)S(1)} %get-tuple-element.54.refs_0_), channel_id=1, source_target_pairs={{0,2},{1,3},{2,0},{3,1},{4,6},{5,7},{6,4},{7,5},{8,10},{9,11},{10,... | collective-permute-start | bytes 12296 | tf_op jit(solution)/shard_map/ppermute | solution.py:27
  35.5 1.7 %left_statistic.1.refs_4_ = f32[256,1024]{1,0:T(8,128)} custom-call(f32[256,1024]{1,0:T(8,128)S(1)} %get-tuple-element.55.old_ref, bf16[256,1024]{1,0:T(8,128)(2,1)S(1)} %join.3.refs_0_.refs_5_, bf16[256,1024]{1,0:T(8,128)(2,1)S(1)} %collective-permute-done.7.refs_1_.refs_6_, bf16[256,1024]{1,0:T(8,128)(2,1)S(1)} %join.4.refs_2_.refs_7_, ...), custom_call_target="tpu_custom_call" | custom-call | flops 536870912 | bytes 4194304 | tf_op jit(solution)/shard_map/left_statistic/pallas_call | solution.py:243
  37.6 1.7 %collective-permute-start.22 = (bf16[32,1024]{1,0:T(8,128)(2,1)S(1)}, bf16[32,1024]{1,0:T(8,128)(2,1)S(1)}, u32[]{:S(2)}, u32[]{:S(2)}) collective-permute-start(bf16[32,1024]{1,0:T(8,128)(2,1)S(1)} %get-tuple-element.60), channel_id=1, source_target_pairs={{0,16},{4,20},{8,24},{12,28},{16,0},{20,4},{24,8},{28,12},{1,17},{... | collective-permute-start | bytes 196616 | tf_op jit(solution)/shard_map/ppermute | solution.py:27
  39.3 1.0 %collective-permute-start.23 = (bf16[32,1024]{1,0:T(8,128)(2,1)S(1)}, bf16[32,1024]{1,0:T(8,128)(2,1)S(1)}, u32[]{:S(2)}, u32[]{:S(2)}) collective-permute-start(bf16[32,1024]{1,0:T(8,128)(2,1)S(1)} %get-tuple-element.61), channel_id=1, source_target_pairs={{0,4},{4,0},{8,12},{12,8},{16,20},{20,16},{24,28},{28,24},{1,5},{5... | collective-permute-start | bytes 196616 | tf_op jit(solution)/shard_map/ppermute | solution.py:27
  40.3 1.8 %collective-permute-start.24 = (bf16[32,1024]{1,0:T(8,128)(2,1)S(1)}, bf16[32,1024]{1,0:T(8,128)(2,1)S(1)}, u32[]{:S(2)}, u32[]{:S(2)}) collective-permute-start(bf16[32,1024]{1,0:T(8,128)(2,1)S(1)} %get-tuple-element.62), channel_id=1, source_target_pairs={{0,20},{4,16},{8,28},{12,24},{16,4},{20,0},{24,12},{28,8},{1,21},{... | collective-permute-start | bytes 196616 | tf_op jit(solution)/shard_map/ppermute | solution.py:27
  42.1 2.2 %collective-permute-start.20 = (bf16[32,1024]{1,0:T(8,128)(2,1)S(1)}, bf16[32,1024]{1,0:T(8,128)(2,1)S(1)}, u32[]{:S(2)}, u32[]{:S(2)}) collective-permute-start(bf16[32,1024]{1,0:T(8,128)(2,1)S(1)} %get-tuple-element.58), channel_id=1, source_target_pairs={{0,24},{4,28},{8,16},{12,20},{16,8},{20,12},{24,0},{28,4},{1,25},{... | collective-permute-start | bytes 196616 | tf_op jit(solution)/shard_map/ppermute | solution.py:27
  45.0 1.9 %collective-permute-start.18 = (bf16[32,1024]{1,0:T(8,128)(2,1)S(1)}, bf16[32,1024]{1,0:T(8,128)(2,1)S(1)}, u32[]{:S(2)}, u32[]{:S(2)}) collective-permute-start(bf16[32,1024]{1,0:T(8,128)(2,1)S(1)} %get-tuple-element.56), channel_id=1, source_target_pairs={{0,28},{4,24},{8,20},{12,16},{16,12},{20,8},{24,4},{28,0},{1,29},{... | collective-permute-start | bytes 196616 | tf_op jit(solution)/shard_map/ppermute | solution.py:27
  47.9 1.4 %collective-permute-done.24.refs_2_ = bf16[32,1024]{1,0:T(8,128)(2,1)S(1)} collective-permute-done((bf16[32,1024]{1,0:T(8,128)(2,1)S(1)}, bf16[32,1024]{1,0:T(8,128)(2,1)S(1)}, u32[]{:S(2)}, u32[]{:S(2)}) %collective-permute-start.24) | collective-permute-done | bytes 65568 | tf_op jit(solution)/shard_map/ppermute | solution.py:27
  49.3 2.2 %update.3 = (f32[32,8192]{1,0:T(8,128)}, f32[32,8192]{1,0:T(8,128)}, bf16[32,8192]{1,0:T(8,128)(2,1)}, f32[256,1024]{1,0:T(8,128)}) custom-call(s32[8,128]{1,0:T(8,128)S(1)} %get-tuple-element.48.block_ref, f32[8,32,1024]{2,1,0:T(8,128)S(1)} %get-tuple-element.49.refs_0_.z_ref, f32[8,32,1024]{2,1,0:T(8,128)S(1)} %get-tuple-element.50.x_ref, ...), custom_call_target="tpu_custom_call" | custom-call | flops 1048576 | bytes 2621440 | tf_op jit(solution)/shard_map/update/pallas_call | solution.py:346
  (42 shorter events, 6.5 us)
Async XLA Ops:
  0.6 25.4 %collective-permute-start.13 = (bf16[256,1024]{1,0:T(8,128)(2,1)}, bf16[256,1024]{1,0:T(8,128)(2,1)S(1)}, u32[]{:S(2)}, u32[]{:S(2)}) collective-permute-start(bf16[256,1024]{1,0:T(8,128)(2,1)} %bitcast.22), channel_id=1, source_target_pairs={{0,2},{1,3},{2,0},{3,1},{4,6},{5,7},{6,4},{7,5},{8,10},{9,11},{10,... | collective-permute-start | bytes 1572872 | tf_op jit(solution)/shard_map/ppermute | solution.py:27
  5.0 7.0 %collective-permute-start = (bf16[32,1024]{1,0:T(8,128)(2,1)S(1)}, bf16[32,1024]{1,0:T(8,128)(2,1)S(1)}, u32[]{:S(2)}, u32[]{:S(2)}) collective-permute-start(bf16[32,1024]{1,0:T(8,128)(2,1)S(1)} %get-tuple-element.40), channel_id=1, source_target_pairs={{0,16},{4,20},{8,24},{12,28},{16,0},{20,4},{24,8},{28,12},{1,17},{... | collective-permute-start | bytes 196616 | tf_op jit(solution)/shard_map/ppermute | solution.py:27
  7.7 7.1 %collective-permute-start.2 = (bf16[32,1024]{1,0:T(8,128)(2,1)S(1)}, bf16[32,1024]{1,0:T(8,128)(2,1)S(1)}, u32[]{:S(2)}, u32[]{:S(2)}) collective-permute-start(bf16[32,1024]{1,0:T(8,128)(2,1)S(1)} %get-tuple-element.42), channel_id=1, source_target_pairs={{0,4},{4,0},{8,12},{12,8},{16,20},{20,16},{24,28},{28,24},{1,5},{5... | collective-permute-start | bytes 196616 | tf_op jit(solution)/shard_map/ppermute | solution.py:27
  9.2 7.7 %collective-permute-start.3 = (bf16[32,1024]{1,0:T(8,128)(2,1)S(1)}, bf16[32,1024]{1,0:T(8,128)(2,1)S(1)}, u32[]{:S(2)}, u32[]{:S(2)}) collective-permute-start(bf16[32,1024]{1,0:T(8,128)(2,1)S(1)} %get-tuple-element.44), channel_id=1, source_target_pairs={{0,12},{4,8},{8,4},{12,0},{16,28},{20,24},{24,20},{28,16},{1,13},{... | collective-permute-start | bytes 196616 | tf_op jit(solution)/shard_map/ppermute | solution.py:27
  10.8 8.6 %collective-permute-start.1 = (bf16[32,1024]{1,0:T(8,128)(2,1)S(1)}, bf16[32,1024]{1,0:T(8,128)(2,1)S(1)}, u32[]{:S(2)}, u32[]{:S(2)}) collective-permute-start(bf16[32,1024]{1,0:T(8,128)(2,1)S(1)} %get-tuple-element.41), channel_id=1, source_target_pairs={{0,20},{4,16},{8,28},{12,24},{16,4},{20,0},{24,12},{28,8},{1,21},{... | collective-permute-start | bytes 196616 | tf_op jit(solution)/shard_map/ppermute | solution.py:27
  12.0 8.0 %collective-permute-start.6 = (bf16[32,1024]{1,0:T(8,128)(2,1)S(1)}, bf16[32,1024]{1,0:T(8,128)(2,1)S(1)}, u32[]{:S(2)}, u32[]{:S(2)}) collective-permute-start(bf16[32,1024]{1,0:T(8,128)(2,1)S(1)} %after.5), channel_id=1, source_target_pairs={{0,24},{4,28},{8,16},{12,20},{16,8},{20,12},{24,0},{28,4},{1,25},{... | collective-permute-start | bytes 196616 | tf_op jit(solution)/shard_map/ppermute | solution.py:27
  14.9 7.1 %collective-permute-start.5 = (bf16[32,1024]{1,0:T(8,128)(2,1)S(1)}, bf16[32,1024]{1,0:T(8,128)(2,1)S(1)}, u32[]{:S(2)}, u32[]{:S(2)}) collective-permute-start(bf16[32,1024]{1,0:T(8,128)(2,1)S(1)} %after.4), channel_id=1, source_target_pairs={{0,28},{4,24},{8,20},{12,16},{16,12},{20,8},{24,4},{28,0},{1,29},{... | collective-permute-start | bytes 196616 | tf_op jit(solution)/shard_map/ppermute | solution.py:27
  16.9 5.0 %collective-permute-start.4 = (bf16[32,1024]{1,0:T(8,128)(2,1)S(1)}, bf16[32,1024]{1,0:T(8,128)(2,1)S(1)}, u32[]{:S(2)}, u32[]{:S(2)}) collective-permute-start(bf16[32,1024]{1,0:T(8,128)(2,1)S(1)} %after.3), channel_id=1, source_target_pairs={{0,8},{4,12},{8,0},{12,4},{16,24},{20,28},{24,16},{28,20},{1,9},{5... | collective-permute-start | bytes 196616 | tf_op jit(solution)/shard_map/ppermute | solution.py:27
  19.5 7.9 %collective-permute-start.8 = (bf16[128,1024]{1,0:T(8,128)(2,1)S(1)}, bf16[128,1024]{1,0:T(8,128)(2,1)S(1)}, u32[]{:S(2)}, u32[]{:S(2)}) collective-permute-start(bf16[128,1024]{1,0:T(8,128)(2,1)S(1)} %half.2.refs_4_.first_ref), channel_id=1, source_target_pairs={{0,2},{1,3},{2,0},{3,1},{4,6},{5,7},{6,4},{7,5},{8,10},{9,11},{10,... | collective-permute-start | bytes 786440 | tf_op jit(solution)/shard_map/ppermute | solution.py:27
  22.0 8.2 %collective-permute-start.9 = (bf16[128,1024]{1,0:T(8,128)(2,1)S(1)}, bf16[128,1024]{1,0:T(8,128)(2,1)S(1)}, u32[]{:S(2)}, u32[]{:S(2)}) collective-permute-start(bf16[128,1024]{1,0:T(8,128)(2,1)S(1)} %half.3.refs_5_.second_ref), channel_id=1, source_target_pairs={{0,2},{1,3},{2,0},{3,1},{4,6},{5,7},{6,4},{7,5},{8,10},{9,11},{10,... | collective-permute-start | bytes 786440 | tf_op jit(solution)/shard_map/ppermute | solution.py:27
  25.4 6.3 %collective-permute-start.12 = (bf16[256,1024]{1,0:T(8,128)(2,1)S(1)}, bf16[256,1024]{1,0:T(8,128)(2,1)S(1)}, u32[]{:S(2)}, u32[]{:S(2)}) collective-permute-start(bf16[256,1024]{1,0:T(8,128)(2,1)S(1)} %get-tuple-element.52.refs_4_), channel_id=1, source_target_pairs={{0,1},{1,0},{2,3},{3,2},{4,5},{5,4},{6,7},{7,6},{8,9},{9,8},{10,11... | collective-permute-start | bytes 1572872 | tf_op jit(solution)/shard_map/ppermute | solution.py:27
  25.5 6.3 %collective-permute-start.7 = (bf16[256,1024]{1,0:T(8,128)(2,1)S(1)}, bf16[256,1024]{1,0:T(8,128)(2,1)S(1)}, u32[]{:S(2)}, u32[]{:S(2)}) collective-permute-start(bf16[256,1024]{1,0:T(8,128)(2,1)S(1)} %join.3.refs_0_.refs_5_), channel_id=1, source_target_pairs={{0,1},{1,0},{2,3},{3,2},{4,5},{5,4},{6,7},{7,6},{8,9},{9,8},{10,11... | collective-permute-start | bytes 1572872 | tf_op jit(solution)/shard_map/ppermute | solution.py:27
  26.0 5.8 %collective-permute-start.14 = (bf16[256,1024]{1,0:T(8,128)(2,1)S(1)}, bf16[256,1024]{1,0:T(8,128)(2,1)S(1)}, u32[]{:S(2)}, u32[]{:S(2)}) collective-permute-start(bf16[256,1024]{1,0:T(8,128)(2,1)S(1)} %collective-permute-done.13.refs_6_), channel_id=1, source_target_pairs={{0,1},{1,0},{2,3},{3,2},{4,5},{5,4},{6,7},{7,6},{8,9},{9,8},{10,11... | collective-permute-start | bytes 1572872 | tf_op jit(solution)/shard_map/ppermute | solution.py:27
  27.4 2.9 %collective-permute-start.10 = (bf16[128,1024]{1,0:T(8,128)(2,1)S(1)}, bf16[128,1024]{1,0:T(8,128)(2,1)S(1)}, u32[]{:S(2)}, u32[]{:S(2)}) collective-permute-start(bf16[128,1024]{1,0:T(8,128)(2,1)S(1)} %collective-permute-done.8.first_ref), channel_id=1, source_target_pairs={{0,1},{1,0},{2,3},{3,2},{4,5},{5,4},{6,7},{7,6},{8,9},{9,8},{10,11... | collective-permute-start | bytes 786440 | tf_op jit(solution)/shard_map/ppermute | solution.py:27
  33.5 3.6 %collective-permute-start.17 = (f32[8,128]{1,0:T(8,128)S(1)}, f32[8,128]{1,0:T(8,128)S(1)}, u32[]{:S(2)}, u32[]{:S(2)}) collective-permute-start(f32[8,128]{1,0:T(8,128)S(1)} %get-tuple-element.54.refs_0_), channel_id=1, source_target_pairs={{0,3},{1,2},{2,1},{3,0},{4,7},{5,6},{6,5},{7,4},{8,11},{9,10},{10,... | collective-permute-start | bytes 12296 | tf_op jit(solution)/shard_map/ppermute | solution.py:27
  33.9 3.6 %collective-permute-start.16 = (f32[8,128]{1,0:T(8,128)S(1)}, f32[8,128]{1,0:T(8,128)S(1)}, u32[]{:S(2)}, u32[]{:S(2)}) collective-permute-start(f32[8,128]{1,0:T(8,128)S(1)} %get-tuple-element.54.refs_0_), channel_id=1, source_target_pairs={{0,2},{1,3},{2,0},{3,1},{4,6},{5,7},{6,4},{7,5},{8,10},{9,11},{10,... | collective-permute-start | bytes 12296 | tf_op jit(solution)/shard_map/ppermute | solution.py:27
  35.4 2.1 %collective-permute-start.15 = (f32[8,128]{1,0:T(8,128)S(1)}, f32[8,128]{1,0:T(8,128)S(1)}, u32[]{:S(2)}, u32[]{:S(2)}) collective-permute-start(f32[8,128]{1,0:T(8,128)S(1)} %get-tuple-element.54.refs_0_), channel_id=1, source_target_pairs={{0,1},{1,0},{2,3},{3,2},{4,5},{5,4},{6,7},{7,6},{8,9},{9,8},{10,11... | collective-permute-start | bytes 12296 | tf_op jit(solution)/shard_map/ppermute | solution.py:27
  37.6 7.4 %collective-permute-start.22 = (bf16[32,1024]{1,0:T(8,128)(2,1)S(1)}, bf16[32,1024]{1,0:T(8,128)(2,1)S(1)}, u32[]{:S(2)}, u32[]{:S(2)}) collective-permute-start(bf16[32,1024]{1,0:T(8,128)(2,1)S(1)} %get-tuple-element.60), channel_id=1, source_target_pairs={{0,16},{4,20},{8,24},{12,28},{16,0},{20,4},{24,8},{28,12},{1,17},{... | collective-permute-start | bytes 196616 | tf_op jit(solution)/shard_map/ppermute | solution.py:27
  39.3 7.6 %collective-permute-start.23 = (bf16[32,1024]{1,0:T(8,128)(2,1)S(1)}, bf16[32,1024]{1,0:T(8,128)(2,1)S(1)}, u32[]{:S(2)}, u32[]{:S(2)}) collective-permute-start(bf16[32,1024]{1,0:T(8,128)(2,1)S(1)} %get-tuple-element.61), channel_id=1, source_target_pairs={{0,4},{4,0},{8,12},{12,8},{16,20},{20,16},{24,28},{28,24},{1,5},{5... | collective-permute-start | bytes 196616 | tf_op jit(solution)/shard_map/ppermute | solution.py:27
  40.3 9.0 %collective-permute-start.24 = (bf16[32,1024]{1,0:T(8,128)(2,1)S(1)}, bf16[32,1024]{1,0:T(8,128)(2,1)S(1)}, u32[]{:S(2)}, u32[]{:S(2)}) collective-permute-start(bf16[32,1024]{1,0:T(8,128)(2,1)S(1)} %get-tuple-element.62), channel_id=1, source_target_pairs={{0,20},{4,16},{8,28},{12,24},{16,4},{20,0},{24,12},{28,8},{1,21},{... | collective-permute-start | bytes 196616 | tf_op jit(solution)/shard_map/ppermute | solution.py:27
  42.1 9.5 %collective-permute-start.20 = (bf16[32,1024]{1,0:T(8,128)(2,1)S(1)}, bf16[32,1024]{1,0:T(8,128)(2,1)S(1)}, u32[]{:S(2)}, u32[]{:S(2)}) collective-permute-start(bf16[32,1024]{1,0:T(8,128)(2,1)S(1)} %get-tuple-element.58), channel_id=1, source_target_pairs={{0,24},{4,28},{8,16},{12,20},{16,8},{20,12},{24,0},{28,4},{1,25},{... | collective-permute-start | bytes 196616 | tf_op jit(solution)/shard_map/ppermute | solution.py:27
  44.3 7.2 %collective-permute-start.21 = (bf16[32,1024]{1,0:T(8,128)(2,1)S(1)}, bf16[32,1024]{1,0:T(8,128)(2,1)S(1)}, u32[]{:S(2)}, u32[]{:S(2)}) collective-permute-start(bf16[32,1024]{1,0:T(8,128)(2,1)S(1)} %get-tuple-element.59), channel_id=1, source_target_pairs={{0,12},{4,8},{8,4},{12,0},{16,28},{20,24},{24,20},{28,16},{1,13},{... | collective-permute-start | bytes 196616 | tf_op jit(solution)/shard_map/ppermute | solution.py:27
  45.0 7.4 %collective-permute-start.18 = (bf16[32,1024]{1,0:T(8,128)(2,1)S(1)}, bf16[32,1024]{1,0:T(8,128)(2,1)S(1)}, u32[]{:S(2)}, u32[]{:S(2)}) collective-permute-start(bf16[32,1024]{1,0:T(8,128)(2,1)S(1)} %get-tuple-element.56), channel_id=1, source_target_pairs={{0,28},{4,24},{8,20},{12,16},{16,12},{20,8},{24,4},{28,0},{1,29},{... | collective-permute-start | bytes 196616 | tf_op jit(solution)/shard_map/ppermute | solution.py:27
  46.9 5.6 %collective-permute-start.19 = (bf16[32,1024]{1,0:T(8,128)(2,1)S(1)}, bf16[32,1024]{1,0:T(8,128)(2,1)S(1)}, u32[]{:S(2)}, u32[]{:S(2)}) collective-permute-start(bf16[32,1024]{1,0:T(8,128)(2,1)S(1)} %get-tuple-element.57), channel_id=1, source_target_pairs={{0,8},{4,12},{8,0},{12,4},{16,24},{20,28},{24,16},{28,20},{1,9},{5... | collective-permute-start | bytes 196616 | tf_op jit(solution)/shard_map/ppermute | solution.py:27
  (1 other events, 1.5 us)
